TPU v7x, 256 devices: a whole 4x4x8 slice. The times are simulated.
256 devices in a mesh: segment: 4 (over x), expert: 16 (over z, core), mp: 4 (over y).
Axes of the slice: x: 4, y: 4, z: 8, core: 2. Of those that a mesh axis runs over, the one named last changes fastest.
Arguments:
- tokens: bfloat16 [4, 2048, 4096], P('segment', 'expert', 'mp'), may hold values from -45 to 45
- routes: int32 [4, 2048, 2], P('segment', 'expert'), may hold values from 0 to 15, all different within a row; in each aligned block of 128 rows (0 to 127, 128 to 255, ..., all dimensions but the last counted through in order) at most 20 rows name the same one
- gate_weights: float32 [4, 2048, 2], P('segment', 'expert'), may hold values from 0.1 to 1
- norm_gain: float32 [4096], replicated, may hold values from 0.25 to 1.75
- gate_proj: bfloat16 [16, 4096, 7168], P('expert', None, ('segment', 'mp')), may hold values from -0.09375 to 0.09375
- up_proj: bfloat16 [16, 4096, 7168], P('expert', None, ('segment', 'mp')), may hold values from -0.09375 to 0.09375
- down_proj: bfloat16 [16, 7168, 4096], P('expert', ('segment', 'mp')), may hold values from -0.09375 to 0.09375
Outputs:
- mixed_out: bfloat16 [4, 2048, 4096], P('segment', 'expert', 'mp')
Inputs may be any that keep to these rules, and one draw needn't show every extreme that they name: `routes`: the 2 experts of a token differ. In each micro-batch, each aligned block of 128 tokens (the tokens of one index of expert) names no expert more than 20 times, and in some blocks one expert exactly 20 times.
All inputs are finite; a program needn't handle non-finite values.
Results may differ from a plain program's by a relative error of at most 0.008.
Values may be sent and summed in bfloat16 or wider, within the bound.
A program may use at most 128 MiB of HBM per device.

v0:
```python
import jax
import jax.numpy as jnp
from jax import lax
from jax.sharding import PartitionSpec as P

EPSILON = 1e-06


def normalize_rows(all_rows, layout, norm_gain, model_parts):
    squares = jnp.einsum(
        layout + "," + layout + "->sr", all_rows, all_rows, preferred_element_type=jnp.float32
    )
    row_scale = lax.rsqrt(squares / norm_gain.shape[0] + EPSILON)
    scaled = (
        all_rows.astype(jnp.float32)
        * row_scale[:, None, :, None]
        * norm_gain.reshape(1, model_parts, 1, -1)
    )
    return scaled.astype(jnp.bfloat16)


def section_terms(all_rows, layout, norm_gain, model_parts, gate_rows, up_rows, down_rows):
    normed = normalize_rows(all_rows, layout, norm_gain, model_parts)
    gate_act = jnp.einsum(
        layout + ",kdh->srh", normed, gate_rows, preferred_element_type=jnp.float32
    )
    up_act = jnp.einsum(layout + ",kdh->srh", normed, up_rows, preferred_element_type=jnp.float32)
    hidden = (jax.nn.silu(gate_act) * up_act).astype(jnp.bfloat16)
    return jnp.einsum("srh,hkd->skrd", hidden, down_rows, preferred_element_type=jnp.float32)


def body(tokens, routes, gate_weights, norm_gain, gate_proj, up_proj, down_proj):
    local_tokens = tokens[0]
    local_routes = routes[0]
    local_gates = gate_weights[0]
    tok_count, feature_part = local_tokens.shape
    top_count = local_routes.shape[1]
    experts = lax.axis_size("expert")
    segments = lax.axis_size("segment")
    model_parts = lax.axis_size("mp")
    capacity = min(tok_count, max(2, 5 * tok_count * top_count // (4 * experts)))
    flat_routes = local_routes.reshape(-1)
    member = (flat_routes[:, None] == jnp.arange(experts, dtype=jnp.int32)[None, :]).astype(
        jnp.int32
    )
    earlier = jnp.cumsum(member, axis=0) - member
    position = jnp.sum(earlier * member, axis=1)
    target = (flat_routes * capacity + position).reshape(tok_count, top_count)
    places = jnp.arange(experts * capacity, dtype=jnp.int32)
    chooser = jnp.any(target[:, :, None] == places[None, None, :], axis=1).astype(jnp.bfloat16)
    outgoing = jnp.einsum(
        "tq,td->qd", chooser, local_tokens, preferred_element_type=jnp.float32
    ).astype(jnp.bfloat16)
    outgoing = outgoing.reshape(experts, capacity, local_tokens.shape[1])
    gate_rows = gate_proj[0].reshape(model_parts, feature_part, -1)
    up_rows = up_proj[0].reshape(model_parts, feature_part, -1)
    down_rows = down_proj[0].reshape(-1, model_parts, feature_part)
    slot_block = lax.all_to_all(outgoing, "expert", split_axis=0, concat_axis=0, tiled=True)
    slot_count = slot_block.shape[1]
    token_rows = slot_block.reshape(-1, slot_block.shape[2])
    all_rows = lax.all_gather(token_rows, ("segment", "mp"), axis=0, tiled=True)
    all_rows = all_rows.reshape(segments, model_parts, -1, feature_part)
    partials = section_terms(
        all_rows, "skrd", norm_gain, model_parts, gate_rows, up_rows, down_rows
    )
    summed = lax.psum_scatter(
        partials.reshape(-1, feature_part).astype(jnp.bfloat16),
        ("segment", "mp"),
        scatter_dimension=0,
        tiled=True,
    )
    expert_out = summed.reshape(experts, slot_count, feature_part)
    returned = lax.all_to_all(expert_out, "expert", split_axis=0, concat_axis=0, tiled=True)
    flat_back = returned.reshape(experts * capacity, feature_part)
    picked = flat_back[target]
    mixed_out = local_tokens.astype(jnp.float32) + jnp.sum(
        local_gates[:, :, None] * picked.astype(jnp.float32), axis=1
    )
    return mixed_out.astype(jnp.bfloat16)[None]


def solution(mesh):
    placed = (
        P("segment", "expert", "mp"),
        P("segment", "expert", None),
        P("segment", "expert", None),
        P(),
        P("expert", None, ("segment", "mp")),
        P("expert", None, ("segment", "mp")),
        P("expert", ("segment", "mp"), None),
    )
    return jax.shard_map(
        body, mesh=mesh, in_specs=placed, out_specs=P("segment", "expert", "mp"), check_vma=False
    )
```

profile of v0, /device:TPU:1, one launch (start us, length us, event | category | flops | bytes accessed | tf_op | source)
XLA Modules:
  0.0 298.9 jit_solution(947042650966476340)
XLA Ops:
  6.5 0.8 copy.20
  7.3 0.1 eq.42
  7.5 0.1 eq.38
  7.6 0.6 reduce-window.6
  8.2 0.2 slice_reduce_fusion
  8.4 0.1 fusion.23
  8.5 0.1 reduce_sum.25
  8.8 1.3 convolution_convert_fusion.1
  10.1 0.1 reshape.82
  10.3 32.7 %all_to_all.10 = bf16[16,20,1024]{2,1,0:T(8,128)(2,1)S(1)} all-to-all(bf16[16,20,1024]{2,1,0:T(8,128)(2,1)S(1)} %reshape.82), channel_id=1, replica_groups=mesh['segment'=4,'expert'=16,'mp'=4] {'expert'}, dimensions={0} | all-to-all | bytes 1310720 | tf_op jit(solution)/shard_map/all_to_all | solution.py:58
  43.0 1.0 reshape.83
  44.0 7.2 %reshape_squeeze.11 = bf16[4,1024,448]{1,0,2:T(4,128)(2,1)} reshape(bf16[1,4096,448]{1,2,0:T(8,128)(2,1)} %param.12) | data formatting | bytes 7340032 | tf_op jit(solution)/shard_map/reshape;squeeze | solution.py:56
  51.2 7.3 %reshape_squeeze.10 = bf16[4,1024,448]{1,0,2:T(4,128)(2,1)} reshape(bf16[1,4096,448]{1,2,0:T(8,128)(2,1)} %param.11) | data formatting | bytes 7340032 | tf_op jit(solution)/shard_map/reshape;squeeze | solution.py:55
  58.5 7.2 %reshape_squeeze.12 = bf16[448,4,1024]{2,1,0:T(4,128)(2,1)} reshape(bf16[1,448,4096]{2,1,0:T(8,128)(2,1)} %param.13) | data formatting | bytes 7340032 | tf_op jit(solution)/shard_map/reshape;squeeze | solution.py:57
  65.7 60.5 %all-gather.2.cloned.1.call-done = bf16[5120,1024]{1,0:T(8,128)(2,1)} async-done(((bf16[320,1024]{1,0:T(8,128)(2,1)}), bf16[5120,1024]{1,0:T(8,128)(2,1)}) %all-gather.2.cloned.1.call-update) | async-done | bytes 10485776 | tf_op jit(solution)/shard_map/all_gather | solution.py:61
  126.3 6.2 %fusion = f32[4,320]{1,0:T(4,128)S(1)} fusion(bf16[4,320,1024,4]{2,1,3,0:T(8,128)(2,1)} %bitcast.89), kind=kLoop, calls=%fused_computation.2 | loop fusion | flops 15727360 | bytes 10490880 | tf_op jit(solution)/shard_map/skrd,skrd->sr/dot_general | solution.py:10
  132.5 0.7 copy-done
  133.2 9.5 %fusion.1 = f32[4,320,448,1]{2,1,3,0:T(8,128)} fusion(bf16[4,4,320,1024]{3,2,1,0:T(8,128)(2,1)S(1)} %bitcast.90, f32[4,1024]{1,0:T(4,128)S(1)} %mul.69, f32[4,320]{1,0:T(4,128)S(1)} %add_rsqrt_fusion, bf16[4,1024,448]{1,0,2:T(4,128)(2,1)} %reshape_squeeze.11), kind=kOutput, calls=%fused_computation.4 | convolution fusion | flops 4718592000 | bytes 16471040 | tf_op jit(solution)/shard_map/skrd,kdh->srh/dot_general | solution.py:27
  142.7 9.7 %fusion.15 = bf16[4,320,448,1]{2,1,3,0:T(8,128)(2,1)S(1)} fusion(f32[4,320,448,1]{2,1,3,0:T(8,128)} %fusion.1, bf16[4,1024,448]{1,0,2:T(4,128)(2,1)S(1)} %copy-done.2, bf16[4,4,320,1024]{3,2,1,0:T(8,128)(2,1)S(1)} %bitcast.91, f32[4,1024]{1,0:T(4,128)S(1)} %mul.69, f32[4,320]{1,0:T(4,128)S(1)} %add_rsqrt_fusion), kind=kOutput, calls=%fused_computation.20 | convolution fusion | flops 4722032640 | bytes 17617920 | tf_op jit(solution)/shard_map/skrd,kdh->srh/dot_general | solution.py:24
  152.4 8.7 %convolution_convert_fusion = bf16[4,320,4,1024]{3,1,2,0:T(8,128)(2,1)} fusion(bf16[4,320,448,1]{2,1,3,0:T(8,128)(2,1)S(1)} %fusion.15, bf16[448,4,1024]{2,1,0:T(4,128)(2,1)S(1)} %copy-done.1), kind=kOutput, calls=%fused_computation.6 | convolution fusion | flops 4702863360 | bytes 15302656 | tf_op jit(solution)/shard_map/srh,hkd->skrd/dot_general | solution.py:29
  161.1 93.7 %reduce-scatter.2.cloned.1.call-done = bf16[320,1024]{1,0:T(8,128)(2,1)} async-done(((bf16[5120,1024]{1,0:T(8,128)(2,1)}), bf16[320,1024]{1,0:T(8,128)(2,1)}) %reduce-scatter.2.cloned.1.call-update) | async-done | bytes 655376 | tf_op jit(solution)/shard_map/reduce_scatter | solution.py:66
  254.8 2.0 reshape.85
  256.8 8.5 %all-to-all-start.1 = ((bf16[16,20,1024]{2,1,0:T(8,128)(2,1)}), bf16[16,20,1024]{2,1,0:T(8,128)(2,1)S(1)}, u32[]{:S(2)}, u32[]{:S(2)}) async-start(bf16[16,20,1024]{2,1,0:T(8,128)(2,1)} %reshape.85), calls=%async_computation.2 | async-start | bytes 1572864 | tf_op jit(solution)/shard_map/all_to_all | solution.py:73
  265.3 0.1 reduce_sum.26
  265.5 0.1 reshape.89
  265.6 0.1 copy.19
  265.7 22.2 %all-to-all-done.1 = bf16[16,20,1024]{2,1,0:T(8,128)(2,1)S(1)} async-done(((bf16[16,20,1024]{2,1,0:T(8,128)(2,1)}), bf16[16,20,1024]{2,1,0:T(8,128)(2,1)S(1)}, u32[]{:S(2)}, u32[]{:S(2)}) %all-to-all-start.1) | async-done | bytes 655392 | tf_op jit(solution)/shard_map/all_to_all | solution.py:73
  288.0 0.1 reshape.86
  288.1 1.2 gather_fusion
  289.3 0.7 reshape.96
  289.9 1.3 multiply_reduce_fusion
  291.3 0.8 fusion.18
  (25 shorter events, 0.3 us)
Async XLA Ops:
  6.5 37.5 %copy-start.4 = (f32[4096]{0:T(1024)S(1)}, f32[4096]{0:T(1024)}, u32[]{:S(2)}) copy-start(f32[4096]{0:T(1024)} %param.10) | copy-start | bytes 49156
  6.5 119.7 %all-gather.2.cloned.1.call-start = ((), (), s32[]{:S(2)}) async-start(), calls=%async_computation.3 | async-start | bytes 11141120 | tf_op jit(solution)/shard_map/all_gather | solution.py:61
  44.0 210.9 %reduce-scatter.2.cloned.1.call-start = ((), (), s32[]{:S(2)}) async-start(), calls=%async_computation.4 | async-start | bytes 11141120 | tf_op jit(solution)/shard_map/reduce_scatter | solution.py:66
  126.2 7.0 %copy-start = (bf16[5120,1024]{1,0:T(8,128)(2,1)S(1)}, bf16[5120,1024]{1,0:T(8,128)(2,1)}, u32[]{:S(2)}) copy-start(bf16[5120,1024]{1,0:T(8,128)(2,1)} %all-gather.2.cloned.1.call-done) | copy-start | bytes 31457284
  133.2 9.5 %copy-start.2 = (bf16[4,1024,448]{1,0,2:T(4,128)(2,1)S(1)}, bf16[4,1024,448]{1,0,2:T(4,128)(2,1)}, u32[]{:S(2)}) copy-start(bf16[4,1024,448]{1,0,2:T(4,128)(2,1)} %reshape_squeeze.10) | copy-start | bytes 11010052
  142.7 9.7 %copy-start.1 = (bf16[448,4,1024]{2,1,0:T(4,128)(2,1)S(1)}, bf16[448,4,1024]{2,1,0:T(4,128)(2,1)}, u32[]{:S(2)}) copy-start(bf16[448,4,1024]{2,1,0:T(4,128)(2,1)} %reshape_squeeze.12) | copy-start | bytes 11010052
  161.1 104.5 %copy-start.5 = (f32[1,128,2]{1,2,0:T(2,128)S(1)}, f32[1,128,2]{1,2,0:T(2,128)}, u32[]{:S(2)}) copy-start(f32[1,128,2]{1,2,0:T(2,128)} %param.9) | copy-start | bytes 3076
  256.8 31.1 %all-to-all-start.1 = ((bf16[16,20,1024]{2,1,0:T(8,128)(2,1)}), bf16[16,20,1024]{2,1,0:T(8,128)(2,1)S(1)}, u32[]{:S(2)}, u32[]{:S(2)}) async-start(bf16[16,20,1024]{2,1,0:T(8,128)(2,1)} %reshape.85), calls=%async_computation.2 | async-start | bytes 1572864 | tf_op jit(solution)/shard_map/all_to_all | solution.py:73
  288.1 3.2 %copy-start.3 = (bf16[1,128,1024]{2,1,0:T(8,128)(2,1)S(1)}, bf16[1,128,1024]{2,1,0:T(8,128)(2,1)}, u32[]{:S(2)}) copy-start(bf16[1,128,1024]{2,1,0:T(8,128)(2,1)} %param.7) | copy-start | bytes 786436
Sparse Core Ops, SparseCore 0:
  44.1 82.1 all-gather.1
  161.2 93.5 reduce-scatter.1
where the time goes:
time: 300 us; the launch traced here: 299 us
  waiting for transfers between devices  177 us (59%)
  blocking collectives  32.7 us (11%)
  local copies, waits for them, and re-layouts  29.3 us (10%)
  matrix products  29.1 us (10%)
  between operations  13.6 us (5%)
  other arithmetic  9.19 us (3%)
  starting transfers between devices  8.5 us (3%)
    reduce_scatter x1, waiting for transfers between devices, body(): lax.psum_scatter(partials.reshape(-1, feature_part).astype(jnp.bfloat16),...  93.7 us
    all_gather x1, waiting for transfers between devices, body(): all_rows = lax.all_gather(token_rows, ('segment', 'mp'), axis=0, tiled=True)  60.5 us
    all_to_all x1, blocking collectives, body(): lax.all_to_all(outgoing, 'expert', split_axis=0, concat_axis=0, tiled=True)  32.7 us
    all_to_all x1, waiting for transfers between devices, body(): lax.all_to_all(expert_out, 'expert', split_axis=0, concat_axis=0, tiled=T...  22.2 us
    dot_general x1, matrix products, section_terms(): jnp.einsum(layout + ',kdh->srh', normed, gate_rows, preferred_element_typ...  9.67 us
    dot_general x1, matrix products, section_terms(): jnp.einsum(layout + ',kdh->srh', normed, up_rows, preferred_element_type=...  9.47 us
    dot_general x1, matrix products, section_terms(): jnp.einsum('srh,hkd->skrd', hidden, down_rows, preferred_element_type=jnp...  8.69 us
    all_to_all x1, starting transfers between devices, body(): lax.all_to_all(expert_out, 'expert', split_axis=0, concat_axis=0, tiled=T...  8.46 us
  transfers between devices with their start and end apart: 3, of which 3 were waited for; matrix products, arithmetic and copies ran while one was open for 7% of the time, Pallas kernels for 0%

commit v1 on v0

v1 whole, which is shorter than its diff:
```python
import functools
import jax
import jax.numpy as jnp
from jax import lax
from jax.experimental import pallas as pl
from jax.experimental.pallas import tpu as pltpu
from jax.sharding import PartitionSpec as P

EPSILON = 1e-06
SLOTS = 4
FOLDS = 4
MESH_IDS = pl.DeviceIdType.MESH

RING = (0, 1, -1, 2)
TURN = {0: -1, 1: 1, -1: -1, 2: 1}


def parent_a(dx, dy):
    if dy in (1, -1):
        return (dx, 0)
    if dy == 2:
        return (dx, TURN[dx])
    return (0, 0) if dx in (1, -1) else (1, 0)


def parent(half, node):
    dx, dy = node
    if half == 0:
        return parent_a(dx, dy)
    py, px = parent_a(dy, dx)
    return (px, py)


def level(node):
    return abs(node[0]) + abs(node[1])


NODES = [(dx, dy) for dx in RING for dy in RING if (dx, dy) != (0, 0)]
NEAR = [n for n in NODES if level(n) == 1]
FAR = [(half, n) for n in NODES if level(n) > 1 for half in (0, 1)]
NEAR_ID = {n: i for i, n in enumerate(NEAR)}
FAR_ID = {m: i for i, m in enumerate(FAR)}
IDS = len(NEAR) + len(FAR)


def children(half, node):
    return [n for h, n in FAR if h == half and parent(half, n) == node]


def depth_below(half, node):
    below = children(half, node)
    return 0 if not below else 1 + max(depth_below(half, n) for n in below)


def step_of(node, up):
    d = (up[0] - node[0], up[1] - node[1])
    return tuple({3: -1, -3: 1}.get(v, v) for v in d)


def kernel(
    dims,
    tokens_ref, routes_ref, gates_ref, gain_ref, gate_hbm, up_hbm, down_hbm,
    out_ref,
    gate_w, up_w, down_w, hidden, rows, parts, far_in, near_in,
    z_out, z_in, b_out, b_in, member, count, chosen_w, chosen_n, total, sq_out, sq_in,
    w_sem, ag_recv, rs_recv, ag_send, rs_send, z_send, z_recv, b_send, b_recv, sq_send, sq_recv,
):
    experts, segments, mps, tok, feat, chunks = dims
    f32, bf16 = jnp.float32, jnp.bfloat16
    fold = feat // FOLDS
    half_w = feat // 2
    per = FOLDS * SLOTS
    slots = experts * per
    block = experts * SLOTS
    hid = hidden.shape[1]
    seg, exp, mp = lax.axis_index("segment"), lax.axis_index("expert"), lax.axis_index("mp")

    def iota(shape, dim):
        return lax.broadcasted_iota(jnp.int32, shape, dim)

    w_copies = [
        pltpu.make_async_copy(src, dst, w_sem.at[i])
        for i, (src, dst) in enumerate(((gate_hbm, gate_w), (up_hbm, up_w), (down_hbm, down_w)))
    ]
    for copy in w_copies:
        copy.start()

    barrier = pltpu.get_barrier_semaphore()

    @pl.loop(1, experts)
    def _(d):
        pl.semaphore_signal(
            barrier, inc=1, device_id={"expert": lax.rem(exp + d, experts)}, device_id_type=MESH_IDS
        )

    for d in range(1, mps):
        pl.semaphore_signal(
            barrier, inc=1, device_id={"mp": lax.rem(mp + d, mps)}, device_id_type=MESH_IDS
        )
    for d in (1, segments - 1):
        pl.semaphore_signal(
            barrier, inc=1, device_id={"segment": lax.rem(seg + d, segments)}, device_id_type=MESH_IDS
        )

    tf = tokens_ref[...].astype(f32)
    sq = tf * tf
    folded = sq[:, 0:128]
    for i in range(1, feat // 128):
        folded = folded + sq[:, i * 128 : (i + 1) * 128]
    mine = jnp.sum(jnp.transpose(folded), axis=0, keepdims=True)
    sq_out[...] = jnp.broadcast_to(mine, (8, tok))
    total[...] = tf

    pl.semaphore_wait(barrier, experts - 1 + mps - 1 + 2)

    sq_copies = []
    for d in range(1, mps):
        copy = pltpu.make_async_remote_copy(
            src_ref=sq_out,
            dst_ref=sq_in.at[d - 1],
            send_sem=sq_send.at[d - 1],
            recv_sem=sq_recv.at[d - 1],
            device_id={"mp": lax.rem(mp + d, mps)},
            device_id_type=MESH_IDS,
        )
        copy.start()
        sq_copies.append(copy)

    row_expert = iota((slots, tok), 0) // per
    first = routes_ref[0:1, :] == row_expert
    second = routes_ref[1:2, :] == row_expert
    named = jnp.logical_or(first, second)
    before = (iota((tok, tok), 0) < iota((tok, tok), 1)).astype(bf16)
    named_f = named.astype(f32)
    earlier = jnp.dot(named_f.astype(bf16), before, preferred_element_type=f32)
    member[...] = named_f
    count[...] = jnp.where(named, earlier, -1.0)
    weight = jnp.where(first, gates_ref[0:1, :], 0.0) + jnp.where(second, gates_ref[1:2, :], 0.0)
    chosen_w[...] = jnp.transpose(weight)
    chosen_n[...] = jnp.transpose(count[...])

    for copy in sq_copies:
        copy.wait_recv()
    squares = sq_out[0:1, :]
    for d in range(mps - 1):
        squares = squares + sq_in[d, 0:1, :]
    scale = lax.rsqrt(squares / (feat * mps) + EPSILON)

    gain_tile = jnp.concatenate(
        [jnp.broadcast_to(gain_ref[mp, g : g + 1, :], (SLOTS, fold)) for g in range(FOLDS)], axis=0
    )
    gain_rows = jnp.concatenate([gain_tile] * experts, axis=0)
    row_fold = lax.rem(iota((slots, tok), 0), per) // SLOTS
    row_slot = lax.rem(iota((slots, tok), 0), SLOTS)

    def z_go(out, got, send, recv, c):
        base = pl.multiple_of(exp * per, per)
        pltpu.make_async_copy(
            out.at[c, pl.ds(base, per), :], got.at[c, pl.ds(base, per), :], recv.at[c]
        ).start()

        @pl.loop(1, experts)
        def _(d):
            other = lax.rem(exp + d, experts)
            pltpu.make_async_remote_copy(
                src_ref=out.at[c, pl.ds(pl.multiple_of(other * per, per), per), :],
                dst_ref=got.at[c, pl.ds(base, per), :],
                send_sem=send.at[c],
                recv_sem=recv.at[c],
                device_id={"expert": other},
                device_id_type=MESH_IDS,
            ).start()

    def dispatch(c):
        fill = jnp.where(count[...] == (row_slot + SLOTS * c).astype(f32), 1.0, 0.0)
        raw = jnp.zeros((slots, fold), f32)
        for g in range(FOLDS):
            pick = jnp.where(row_fold == g, fill, 0.0).astype(bf16)
            raw = raw + jnp.dot(
                pick, tokens_ref[:, g * fold : (g + 1) * fold], preferred_element_type=f32
            )
        row_scale = jnp.sum(fill * scale, axis=1, keepdims=True)
        z_out[c] = (raw * row_scale * gain_rows).astype(bf16)
        z_go(z_out, z_in, z_send, z_recv, c)

    def sign(c):
        return 1 - 2 * lax.rem(c, 2)

    def origin(c, node):
        s = sign(c)
        ox = lax.rem(seg + 2 * segments - s * node[0], segments)
        oy = lax.rem(mp + 2 * mps - s * node[1], mps)
        return ox, oy

    def spot(c, node, half=None):
        ox, oy = origin(c, node)
        r = pl.ds(pl.multiple_of(ox * block, block), block)
        if half is None:
            return r, pl.ds(pl.multiple_of(oy * feat, feat), feat)
        return r, pl.ds(pl.multiple_of(oy * feat + half * half_w, half_w), half_w)

    def hop(c, move):
        s = sign(c)
        if move[0] != 0:
            return {"segment": lax.rem(seg + segments + s * move[0], segments)}
        return {"mp": lax.rem(mp + mps + s * move[1], mps)}

    def send_near(c):
        r, f = spot(c, (0, 0))
        for node in NEAR:
            pltpu.make_async_remote_copy(
                src_ref=rows.at[c, r, f],
                dst_ref=rows.at[c, r, f],
                send_sem=ag_send.at[c],
                recv_sem=ag_recv.at[c, NEAR_ID[node]],
                device_id=hop(c, node),
                device_id_type=MESH_IDS,
            ).start()

    def wait_rows(c, lev):
        if lev == 1:
            for node in NEAR:
                r, f = spot(c, node)
                at = rows.at[c, r, f]
                pltpu.make_async_copy(at, at, ag_recv.at[c, NEAR_ID[node]]).wait()
        else:
            for half, node in FAR:
                if level(node) == lev:
                    r, f = spot(c, node, half)
                    at = rows.at[c, r, f]
                    pltpu.make_async_copy(at, at, ag_recv.at[c, len(NEAR) + FAR_ID[half, node]]).wait()

    def send_rows(c, lev):
        for half, node in FAR:
            up = parent(half, node)
            if level(up) == lev:
                r, f = spot(c, up, half)
                pltpu.make_async_remote_copy(
                    src_ref=rows.at[c, r, f],
                    dst_ref=rows.at[c, r, f],
                    send_sem=ag_send.at[c],
                    recv_sem=ag_recv.at[c, len(NEAR) + FAR_ID[half, node]],
                    device_id=hop(c, step_of(up, node)),
                    device_id_type=MESH_IDS,
                ).start()

    def unfold(c):
        pltpu.make_async_copy(z_in.at[c], z_in.at[c], z_recv.at[c]).wait()
        got = z_in[c]
        r_, q_ = iota((block, slots), 0), iota((block, slots), 1)
        place = (r_ // SLOTS) * per + lax.rem(r_, SLOTS)
        ox = pl.multiple_of(seg * block, block)
        for g in range(FOLDS):
            pick = jnp.where(q_ == place + g * SLOTS, 1.0, 0.0).astype(bf16)
            rows[c, pl.ds(ox, block), pl.ds(pl.multiple_of(mp * feat + g * fold, fold), fold)] = (
                jnp.dot(pick, got, preferred_element_type=f32).astype(bf16)
            )
        send_near(c)

    nt = (((1,), (1,)), ((), ()))

    def compute(c):
        x = rows[c]
        gate = lax.dot_general(x, gate_w[...], nt, preferred_element_type=f32)
        up = lax.dot_general(x, up_w[...], nt, preferred_element_type=f32)
        hidden[...] = (gate / (1.0 + jnp.exp(-gate)) * up).astype(bf16)

        @pl.loop(0, mps * 2)
        def _(i):
            cols = pl.ds(pl.multiple_of(i * half_w, half_w), half_w)
            parts[c, :, cols] = jnp.dot(
                hidden[...], down_w[:, cols], preferred_element_type=f32
            ).astype(bf16)

    def add_up(c, half, node):
        r, f = spot(c, node, half)
        acc = parts[c, r, f].astype(f32)
        for n in children(half, node):
            i = FAR_ID[half, n]
            at = far_in.at[c, i]
            pltpu.make_async_copy(at, at, rs_recv.at[c, len(NEAR) + i]).wait()
            acc = acc + far_in[c, i].astype(f32)
        parts[c, r, f] = acc.astype(bf16)

    def send_far(c, half, node):
        r, f = spot(c, node, half)
        i = FAR_ID[half, node]
        pltpu.make_async_remote_copy(
            src_ref=parts.at[c, r, f],
            dst_ref=far_in.at[c, i],
            send_sem=rs_send.at[c],
            recv_sem=rs_recv.at[c, len(NEAR) + i],
            device_id=hop(c, step_of(node, parent(half, node))),
            device_id_type=MESH_IDS,
        ).start()

    def sums_at(c, below):
        for half, node in FAR:
            if depth_below(half, node) == below:
                if below:
                    add_up(c, half, node)
                send_far(c, half, node)

    def sums_near(c):
        for node in NEAR:
            for half in (0, 1):
                if children(half, node):
                    add_up(c, half, node)
            r, f = spot(c, node)
            pltpu.make_async_remote_copy(
                src_ref=parts.at[c, r, f],
                dst_ref=near_in.at[c, NEAR_ID[node]],
                send_sem=rs_send.at[c],
                recv_sem=rs_recv.at[c, NEAR_ID[node]],
                device_id=hop(c, (-node[0], -node[1])),
                device_id_type=MESH_IDS,
            ).start()

    def finish(c):
        r, _ = spot(c, (0, 0))
        for i in range(len(NEAR)):
            at = near_in.at[c, i]
            pltpu.make_async_copy(at, at, rs_recv.at[c, i]).wait()
        q_, r_ = iota((slots, block), 0), iota((slots, block), 1)
        place = (r_ // SLOTS) * per + lax.rem(r_, SLOTS)
        back = jnp.zeros((slots, fold), f32)
        for g in range(FOLDS):
            acc = parts[c, r, pl.ds(pl.multiple_of(mp * feat + g * fold, fold), fold)].astype(f32)
            for i in range(len(NEAR)):
                acc = acc + near_in[c, i, :, g * fold : (g + 1) * fold].astype(f32)
            pick = jnp.where(q_ == place + g * SLOTS, 1.0, 0.0).astype(bf16)
            back = back + jnp.dot(pick, acc.astype(bf16), preferred_element_type=f32)
        b_out[c] = back.astype(bf16)
        z_go(b_out, b_in, b_send, b_recv, c)

    lane_fold = lax.rem(iota((tok, slots), 1), per) // SLOTS
    lane_slot = lax.rem(iota((tok, slots), 1), SLOTS)

    def combine(c):
        pltpu.make_async_copy(b_in.at[c], b_in.at[c], b_recv.at[c]).wait()
        got = b_in[c]
        share = jnp.where(chosen_n[...] == (lane_slot + SLOTS * c).astype(f32), chosen_w[...], 0.0)
        for g in range(FOLDS):
            part = jnp.where(lane_fold == g, share, 0.0)
            high = part.astype(bf16)
            low = (part - high.astype(f32)).astype(bf16)
            cols = slice(g * fold, (g + 1) * fold)
            total[:, cols] += jnp.dot(high, got, preferred_element_type=f32) + jnp.dot(
                low, got, preferred_element_type=f32
            )

    dispatch(0)
    dispatch(1)
    unfold(0)

    @pl.loop(2, chunks)
    def _(c):
        dispatch(c)

    for copy in w_copies:
        copy.wait()

    @pl.loop(0, chunks + 3)
    def _(t):
        def stage(lag, act):
            c = t - lag
            pl.when(jnp.logical_and(c >= 0, c < chunks))(lambda: act(c))

        @functools.partial(stage, 0)
        def _(c):
            wait_rows(c, 1)
            send_rows(c, 1)

        stage(2, sums_near)
        stage(-1, lambda c: pl.when(c >= 1)(lambda: unfold(c)))

        @functools.partial(stage, 1)
        def _(c):
            wait_rows(c, 4)
            compute(c)
            sums_at(c, 0)

        @functools.partial(stage, 0)
        def _(c):
            wait_rows(c, 2)
            send_rows(c, 2)

        stage(2, finish)
        stage(1, lambda c: sums_at(c, 1))

        @functools.partial(stage, 0)
        def _(c):
            wait_rows(c, 3)
            send_rows(c, 3)

        stage(1, lambda c: sums_at(c, 2))
        stage(3, combine)

    out_ref[...] = total[...].astype(bf16)

    for copy in sq_copies:
        copy.wait_send()
    sent = segments * mps - 1
    tall = sent * block // mps

    @pl.loop(0, chunks)
    def _(c):
        for ref, sem in ((rows, ag_send), (parts, rs_send)):
            at = ref.at[c, 0:tall, :]
            pltpu.make_async_copy(at, at, sem.at[c]).wait()
        for ref, sem in ((z_out, z_send), (b_out, b_send)):
            at = ref.at[c, 0 : slots - per, :]
            pltpu.make_async_copy(at, at, sem.at[c]).wait()


def body(tokens, routes, gate_weights, norm_gain, gate_proj, up_proj, down_proj):
    experts, segments, mps = (lax.axis_size(a) for a in ("expert", "segment", "mp"))
    tok, feat = tokens.shape[1:]
    capacity = min(tok, 20)
    chunks = -(-capacity // SLOTS)
    fold = feat // FOLDS
    slots = experts * FOLDS * SLOTS
    block = experts * SLOTS
    hid = down_proj.shape[1]
    width = feat * mps
    dims = (experts, segments, mps, tok, feat, chunks)
    bf16, f32 = jnp.bfloat16, jnp.float32
    vmem, dma = pltpu.VMEM, pltpu.SemaphoreType.DMA
    out = pl.pallas_call(
        functools.partial(kernel, dims),
        out_shape=jax.ShapeDtypeStruct((tok, feat), bf16),
        in_specs=[pl.BlockSpec(memory_space=pltpu.VMEM)] * 4 + [pl.BlockSpec(memory_space=pl.ANY)] * 3,
        out_specs=pl.BlockSpec(memory_space=pltpu.VMEM),
        scratch_shapes=[
            vmem((hid, width), bf16),
            vmem((hid, width), bf16),
            vmem((hid, width), bf16),
            vmem((segments * block, hid), bf16),
            vmem((chunks, segments * block, width), bf16),
            vmem((chunks, segments * block, width), bf16),
            vmem((chunks, len(FAR), block, feat // 2), bf16),
            vmem((chunks, len(NEAR), block, feat), bf16),
            vmem((chunks, slots, fold), bf16),
            vmem((chunks, slots, fold), bf16),
            vmem((chunks, slots, fold), bf16),
            vmem((chunks, slots, fold), bf16),
            vmem((slots, tok), f32),
            vmem((slots, tok), f32),
            vmem((tok, slots), f32),
            vmem((tok, slots), f32),
            vmem((tok, feat), f32),
            vmem((8, tok), f32),
            vmem((mps - 1, 8, tok), f32),
            dma((3,)),
            dma((chunks, IDS)),
            dma((chunks, IDS)),
            dma((chunks,)),
            dma((chunks,)),
            dma((chunks,)),
            dma((chunks,)),
            dma((chunks,)),
            dma((chunks,)),
            dma((mps - 1,)),
            dma((mps - 1,)),
        ],
        compiler_params=pltpu.CompilerParams(
            collective_id=0, has_side_effects=True, vmem_limit_bytes=60 * 1024 * 1024
        ),
        cost_estimate=pl.CostEstimate(
            flops=6 * chunks * segments * block * width * hid,
            bytes_accessed=6 * width * hid,
            transcendentals=chunks * segments * block * hid,
        ),
        name="expert_block",
    )(
        tokens[0],
        jnp.swapaxes(routes, 1, 2)[0],
        jnp.swapaxes(gate_weights, 1, 2)[0],
        norm_gain.reshape(mps, FOLDS, fold),
        jnp.swapaxes(gate_proj, 1, 2)[0],
        jnp.swapaxes(up_proj, 1, 2)[0],
        down_proj[0],
    )
    return out[None]


def solution(mesh):
    placed = (
        P("segment", "expert", "mp"),
        P("segment", "expert", None),
        P("segment", "expert", None),
        P(),
        P("expert", None, ("segment", "mp")),
        P("expert", None, ("segment", "mp")),
        P("expert", ("segment", "mp"), None),
    )
    return jax.shard_map(
        body, mesh=mesh, in_specs=placed, out_specs=P("segment", "expert", "mp"), check_vma=False
    )
```

time: 300 us -> 166 us (0.55)
  waiting for transfers between devices: 177 us -> 0 us
  Pallas kernels: 0 us -> 162 us
  blocking collectives: 32.7 us -> 0 us
  matrix products: 29.1 us -> 0 us
  local copies, waits for them, and re-layouts: 29.3 us -> 3 us
  between operations: 13.6 us -> 0.01 us
  other arithmetic: 9.19 us -> 0 us
  starting transfers between devices: 8.5 us -> 0 us
    pallas_call x0 -> x1, Pallas kernels: none -> 162 us  [body(): pl.pallas_call(functools.partial(kernel, dims), out_shape=jax.ShapeDtypeS...]
    reduce_scatter x1 -> x0, waiting for transfers between devices: 93.7 us -> none  [body(): lax.psum_scatter(partials.reshape(-1, feature_part).astype(jnp.bfloat16),...]
    all_gather x1 -> x0, waiting for transfers between devices: 60.5 us -> none  [body(): all_rows = lax.all_gather(token_rows, ('segment', 'mp'), axis=0, tiled=True)]
    all_to_all x1 -> x0, blocking collectives: 32.7 us -> none  [body(): lax.all_to_all(outgoing, 'expert', split_axis=0, concat_axis=0, tiled=True)]
    dot_general x4 -> x0, matrix products: 29.1 us -> none  [the longest x1 9.67 us: section_terms(): jnp.einsum(layout + ',kdh->srh', normed, gate_rows, preferred_element_typ...]
    all_to_all x1 -> x0, waiting for transfers between devices: 22.2 us -> none  [body(): lax.all_to_all(expert_out, 'expert', split_axis=0, concat_axis=0, tiled=T...]
    another operation x4 -> x0, local copies, waits for them, and re-layouts: 21.7 us -> none  [the longest x1 7.29 us: body(): gate_rows = gate_proj[0].reshape(model_parts, feature_part, -1)]
    all_to_all x1 -> x0, starting transfers between devices: 8.46 us -> none  [body(): lax.all_to_all(expert_out, 'expert', split_axis=0, concat_axis=0, tiled=T...]
  transfers between devices with their start and end apart: 3 -> 0, of which waited for: 3 -> 0; matrix products, arithmetic and copies ran while one was open for 7% -> 0% of each run, Pallas kernels for 0% -> 0%
where the time goes in v1:
time: 166 us; the launch traced here: 165 us
  Pallas kernels  162 us (98%)
  local copies, waits for them, and re-layouts  3 us (2%)
    pallas_call x1, Pallas kernels, body(): pl.pallas_call(functools.partial(kernel, dims), out_shape=jax.ShapeDtypeS...  162 us

profile of v1, /device:TPU:1, one launch (start us, length us, event | category | flops | bytes accessed | tf_op | source)
XLA Modules:
  0.0 165.3 jit_solution(15789943410953265334)
XLA Ops:
  0.0 1.3 reshape.3.gain_ref
  1.3 162.2 %expert_block.1 = bf16[128,1024]{1,0:T(8,128)(2,1)} custom-call(bf16[128,1024]{1,0:T(8,128)(2,1)} %bitcast.19, s32[2,128]{1,0:T(2,128)} %bitcast.20, f32[2,128]{1,0:T(2,128)} %bitcast.21, f32[4,4,256]{2,1,0:T(4,128)} %reshape.3.gain_ref, bf16[448,4096]{1,0:T(8,128)(2,1)} %bitcast.16, bf16[448,4096]{1,0:T(8,128)(2,1)} %bitcast.17, bf16[448,4096]{1,0:T(8,128)(2,1)} %bitcast.18), custom_call_target="tpu_custom_call" | custom-call | flops 14092861440 | bytes 11010048 | tf_op jit(solution)/shard_map/expert_block/pallas_call | solution.py:429
  163.6 1.7 %copy.9 = bf16[1,128,1024]{2,1,0:T(8,128)(2,1)} copy(bf16[1,128,1024]{2,1,0:T(8,128)(2,1)} %bitcast.15) | data formatting | bytes 524288

commit v2 on v1

--- a/solution.py
+++ b/solution.py
@@ -57,13 +57,49 @@
     return tuple({3: -1, -3: 1}.get(v, v) for v in d)
 
 
+ORDER = (
+    ("z", 0), ("z", 1), ("fold",), ("uf", 0), ("uf", 1), ("z", 2), ("z", 3), ("fn", 0, (0, 1)),
+    ("fn", 0, (0, -1)), ("fn", 0, (1, 0)), ("fn", 0, (-1, 0)), ("z", 4), ("fn", 1, (0, -1)), ("fn", 1, (0, 1)),
+    ("ff", 0, 1, (0, 2)), ("ff", 0, 1, (1, 1)), ("fn", 1, (1, 0)), ("ff", 0, 0, (1, 1)), ("ff", 0, 1, (-1, -1)),
+    ("fn", 1, (-1, 0)), ("ff", 0, 0, (-1, -1)), ("ff", 0, 0, (2, 0)), ("ff", 1, 1, (0, 2)),
+    ("ff", 1, 1, (-1, -1)), ("ff", 1, 0, (1, 1)), ("ff", 1, 1, (1, 1)), ("uf", 2), ("ff", 0, 1, (1, 2)),
+    ("ff", 1, 0, (-1, -1)), ("ff", 1, 0, (2, 0)), ("ff", 0, 0, (2, 1)), ("uf", 3), ("ff", 1, 1, (1, 2)),
+    ("uf", 4), ("fn", 2, (0, 1)), ("fn", 2, (0, -1)), ("ff", 1, 0, (2, 1)), ("fn", 2, (1, 0)),
+    ("fn", 2, (-1, 0)), ("gu", 0), ("dn", 0, 2), ("dn", 0, 1), ("dn", 0, -1), ("dn", 0, 0),
+    ("ff", 2, 1, (0, 2)), ("ff", 2, 1, (1, 1)), ("fn", 3, (0, 1)), ("ff", 2, 0, (1, 1)), ("ff", 2, 1, (-1, -1)),
+    ("fn", 3, (0, -1)), ("ff", 2, 0, (-1, -1)), ("ff", 2, 0, (2, 0)), ("fn", 3, (1, 0)), ("fn", 3, (-1, 0)),
+    ("gu", 1), ("dn", 1, 2), ("dn", 1, 1), ("dn", 1, -1), ("dn", 1, 0), ("ff", 3, 1, (0, 2)),
+    ("ff", 3, 1, (1, 1)), ("ff", 2, 1, (1, 2)), ("rf", 0, 1, (1, 2)), ("rf", 0, 0, (1, 1)),
+    ("rf", 0, 1, (1, 1)), ("rf", 0, 0, (2, 1)), ("rf", 0, 0, (-1, -1)), ("rf", 0, 1, (-1, -1)),
+    ("ff", 3, 0, (1, 1)), ("ff", 2, 0, (2, 1)), ("fn", 4, (0, 1)), ("ff", 3, 1, (-1, -1)), ("ff", 3, 0, (2, 0)),
+    ("ff", 3, 0, (-1, -1)), ("fn", 4, (0, -1)), ("fn", 4, (1, 0)), ("fn", 4, (-1, 0)), ("rf", 1, 0, (1, 1)),
+    ("rf", 1, 1, (1, 2)), ("rf", 1, 0, (-1, -1)), ("rf", 1, 0, (2, 1)), ("rf", 1, 1, (1, 1)),
+    ("rf", 1, 1, (-1, -1)), ("ff", 3, 1, (1, 2)), ("rn", 0, (-1, 0)), ("rf", 0, 0, (2, 0)),
+    ("ff", 4, 1, (0, 2)), ("rf", 0, 1, (0, 2)), ("rn", 0, (0, -1)), ("ff", 4, 1, (1, 1)), ("ff", 3, 0, (2, 1)),
+    ("gu", 2), ("dn", 2, 2), ("dn", 2, 1), ("dn", 2, -1), ("dn", 2, 0), ("ff", 4, 0, (1, 1)),
+    ("ff", 4, 0, (-1, -1)), ("ff", 4, 1, (-1, -1)), ("ff", 4, 0, (2, 0)), ("rf", 1, 1, (0, 2)),
+    ("rf", 1, 0, (2, 0)), ("rn", 0, (0, 1)), ("rn", 0, (1, 0)), ("rn", 1, (0, -1)), ("rf", 2, 0, (1, 1)),
+    ("rn", 1, (-1, 0)), ("ff", 4, 1, (1, 2)), ("rf", 2, 1, (1, 2)), ("rf", 2, 0, (2, 1)), ("gu", 3),
+    ("dn", 3, 2), ("dn", 3, 1), ("dn", 3, -1), ("dn", 3, 0), ("ff", 4, 0, (2, 1)), ("rf", 2, 1, (1, 1)),
+    ("rf", 2, 0, (-1, -1)), ("rf", 2, 1, (-1, -1)), ("fi", 0), ("rf", 3, 0, (1, 1)), ("rn", 1, (0, 1)),
+    ("rn", 1, (1, 0)), ("rf", 2, 1, (0, 2)), ("rf", 3, 1, (1, 2)), ("rf", 3, 0, (2, 1)), ("rf", 2, 0, (2, 0)),
+    ("rf", 3, 1, (1, 1)), ("gu", 4), ("dn", 4, 2), ("dn", 4, 1), ("dn", 4, -1), ("dn", 4, 0),
+    ("rf", 3, 1, (0, 2)), ("rf", 3, 0, (-1, -1)), ("rf", 3, 1, (-1, -1)), ("rf", 3, 0, (2, 0)), ("fi", 1),
+    ("rf", 4, 1, (1, 2)), ("rf", 4, 0, (1, 1)), ("rf", 4, 1, (1, 1)), ("rf", 4, 0, (2, 1)),
+    ("rf", 4, 0, (-1, -1)), ("rn", 2, (0, 1)), ("rf", 4, 1, (-1, -1)), ("rn", 2, (0, -1)), ("rn", 2, (1, 0)),
+    ("rf", 4, 1, (0, 2)), ("rn", 2, (-1, 0)), ("rf", 4, 0, (2, 0)), ("rn", 3, (0, 1)), ("rn", 3, (0, -1)),
+    ("rn", 3, (1, 0)), ("rn", 3, (-1, 0)), ("rn", 4, (0, -1)), ("rn", 4, (-1, 0)), ("fi", 2), ("rn", 4, (0, 1)),
+    ("rn", 4, (1, 0)), ("fi", 3), ("fi", 4), ("co", 0), ("co", 1), ("co", 2), ("co", 3), ("co", 4),
+)
+
+
 def kernel(
     dims,
     tokens_ref, routes_ref, gates_ref, gain_ref, gate_hbm, up_hbm, down_hbm,
     out_ref,
     gate_w, up_w, down_w, hidden, rows, parts, far_in, near_in,
-    z_out, z_in, b_out, b_in, member, count, chosen_w, chosen_n, total, sq_out, sq_in,
-    w_sem, ag_recv, rs_recv, ag_send, rs_send, z_send, z_recv, b_send, b_recv, sq_send, sq_recv,
+    z_out, z_in, b_out, b_in, count, chosen_w, chosen_n, total,
+    w_sem, ag_recv, rs_recv, ag_send, rs_send, z_send, z_recv, b_send, b_recv,
 ):
     experts, segments, mps, tok, feat, chunks = dims
     f32, bf16 = jnp.float32, jnp.bfloat16
@@ -72,18 +108,10 @@
     per = FOLDS * SLOTS
     slots = experts * per
     block = experts * SLOTS
-    hid = hidden.shape[1]
     seg, exp, mp = lax.axis_index("segment"), lax.axis_index("expert"), lax.axis_index("mp")
 
     def iota(shape, dim):
         return lax.broadcasted_iota(jnp.int32, shape, dim)
-
-    w_copies = [
-        pltpu.make_async_copy(src, dst, w_sem.at[i])
-        for i, (src, dst) in enumerate(((gate_hbm, gate_w), (up_hbm, up_w), (down_hbm, down_w)))
-    ]
-    for copy in w_copies:
-        copy.start()
 
     barrier = pltpu.get_barrier_semaphore()
 
@@ -93,7 +121,7 @@
             barrier, inc=1, device_id={"expert": lax.rem(exp + d, experts)}, device_id_type=MESH_IDS
         )
 
-    for d in range(1, mps):
+    for d in (1, mps - 1):
         pl.semaphore_signal(
             barrier, inc=1, device_id={"mp": lax.rem(mp + d, mps)}, device_id_type=MESH_IDS
         )
@@ -102,56 +130,35 @@
             barrier, inc=1, device_id={"segment": lax.rem(seg + d, segments)}, device_id_type=MESH_IDS
         )
 
-    tf = tokens_ref[...].astype(f32)
-    sq = tf * tf
-    folded = sq[:, 0:128]
-    for i in range(1, feat // 128):
-        folded = folded + sq[:, i * 128 : (i + 1) * 128]
-    mine = jnp.sum(jnp.transpose(folded), axis=0, keepdims=True)
-    sq_out[...] = jnp.broadcast_to(mine, (8, tok))
-    total[...] = tf
-
-    pl.semaphore_wait(barrier, experts - 1 + mps - 1 + 2)
-
-    sq_copies = []
-    for d in range(1, mps):
-        copy = pltpu.make_async_remote_copy(
-            src_ref=sq_out,
-            dst_ref=sq_in.at[d - 1],
-            send_sem=sq_send.at[d - 1],
-            recv_sem=sq_recv.at[d - 1],
-            device_id={"mp": lax.rem(mp + d, mps)},
-            device_id_type=MESH_IDS,
-        )
+    w_copies = [
+        pltpu.make_async_copy(src, dst, w_sem.at[i])
+        for i, (src, dst) in enumerate(((gate_hbm, gate_w), (up_hbm, up_w), (down_hbm, down_w)))
+    ]
+    for copy in w_copies:
         copy.start()
-        sq_copies.append(copy)
-
-    row_expert = iota((slots, tok), 0) // per
-    first = routes_ref[0:1, :] == row_expert
-    second = routes_ref[1:2, :] == row_expert
+
+    row = iota((slots, tok), 0)
+    first = routes_ref[0:1, :] == row // per
+    second = routes_ref[1:2, :] == row // per
     named = jnp.logical_or(first, second)
     before = (iota((tok, tok), 0) < iota((tok, tok), 1)).astype(bf16)
-    named_f = named.astype(f32)
-    earlier = jnp.dot(named_f.astype(bf16), before, preferred_element_type=f32)
-    member[...] = named_f
+    earlier = jnp.dot(named.astype(f32).astype(bf16), before, preferred_element_type=f32)
     count[...] = jnp.where(named, earlier, -1.0)
-    weight = jnp.where(first, gates_ref[0:1, :], 0.0) + jnp.where(second, gates_ref[1:2, :], 0.0)
-    chosen_w[...] = jnp.transpose(weight)
-    chosen_n[...] = jnp.transpose(count[...])
-
-    for copy in sq_copies:
-        copy.wait_recv()
-    squares = sq_out[0:1, :]
-    for d in range(mps - 1):
-        squares = squares + sq_in[d, 0:1, :]
-    scale = lax.rsqrt(squares / (feat * mps) + EPSILON)
-
-    gain_tile = jnp.concatenate(
-        [jnp.broadcast_to(gain_ref[mp, g : g + 1, :], (SLOTS, fold)) for g in range(FOLDS)], axis=0
-    )
-    gain_rows = jnp.concatenate([gain_tile] * experts, axis=0)
-    row_fold = lax.rem(iota((slots, tok), 0), per) // SLOTS
-    row_slot = lax.rem(iota((slots, tok), 0), SLOTS)
+    row_fold = lax.rem(row, per) // SLOTS
+    row_slot = lax.rem(row, SLOTS)
+
+    @pl.loop(0, chunks)
+    def _(c):
+        fill = jnp.where(count[...] == (row_slot + SLOTS * c).astype(f32), 1.0, 0.0)
+        picked = jnp.zeros((slots, fold), f32)
+        for g in range(FOLDS):
+            pick = jnp.where(row_fold == g, fill, 0.0).astype(bf16)
+            picked = picked + jnp.dot(
+                pick, tokens_ref[:, g * fold : (g + 1) * fold], preferred_element_type=f32
+            )
+        z_out[c] = picked.astype(bf16)
+
+    pl.semaphore_wait(barrier, experts - 1 + 4)
 
     def z_go(out, got, send, recv, c):
         base = pl.multiple_of(exp * per, per)
@@ -171,20 +178,8 @@
                 device_id_type=MESH_IDS,
             ).start()
 
-    def dispatch(c):
-        fill = jnp.where(count[...] == (row_slot + SLOTS * c).astype(f32), 1.0, 0.0)
-        raw = jnp.zeros((slots, fold), f32)
-        for g in range(FOLDS):
-            pick = jnp.where(row_fold == g, fill, 0.0).astype(bf16)
-            raw = raw + jnp.dot(
-                pick, tokens_ref[:, g * fold : (g + 1) * fold], preferred_element_type=f32
-            )
-        row_scale = jnp.sum(fill * scale, axis=1, keepdims=True)
-        z_out[c] = (raw * row_scale * gain_rows).astype(bf16)
-        z_go(z_out, z_in, z_send, z_recv, c)
-
     def sign(c):
-        return 1 - 2 * lax.rem(c, 2)
+        return 1 - 2 * (c % 2)
 
     def origin(c, node):
         s = sign(c)
@@ -217,32 +212,33 @@
                 device_id_type=MESH_IDS,
             ).start()
 
-    def wait_rows(c, lev):
-        if lev == 1:
-            for node in NEAR:
-                r, f = spot(c, node)
-                at = rows.at[c, r, f]
-                pltpu.make_async_copy(at, at, ag_recv.at[c, NEAR_ID[node]]).wait()
-        else:
-            for half, node in FAR:
-                if level(node) == lev:
-                    r, f = spot(c, node, half)
-                    at = rows.at[c, r, f]
-                    pltpu.make_async_copy(at, at, ag_recv.at[c, len(NEAR) + FAR_ID[half, node]]).wait()
-
-    def send_rows(c, lev):
-        for half, node in FAR:
-            up = parent(half, node)
-            if level(up) == lev:
-                r, f = spot(c, up, half)
-                pltpu.make_async_remote_copy(
-                    src_ref=rows.at[c, r, f],
-                    dst_ref=rows.at[c, r, f],
-                    send_sem=ag_send.at[c],
-                    recv_sem=ag_recv.at[c, len(NEAR) + FAR_ID[half, node]],
-                    device_id=hop(c, step_of(up, node)),
-                    device_id_type=MESH_IDS,
-                ).start()
+    def pass_on(c, half, node):
+        for n in children(half, node):
+            r, f = spot(c, node, half)
+            pltpu.make_async_remote_copy(
+                src_ref=rows.at[c, r, f],
+                dst_ref=rows.at[c, r, f],
+                send_sem=ag_send.at[c],
+                recv_sem=ag_recv.at[c, len(NEAR) + FAR_ID[half, n]],
+                device_id=hop(c, step_of(node, n)),
+                device_id_type=MESH_IDS,
+            ).start()
+
+    def wait_far(c, half, node):
+        r, f = spot(c, node, half)
+        at = rows.at[c, r, f]
+        pltpu.make_async_copy(at, at, ag_recv.at[c, len(NEAR) + FAR_ID[half, node]]).wait()
+
+    def from_near(c, node):
+        r, f = spot(c, node)
+        at = rows.at[c, r, f]
+        pltpu.make_async_copy(at, at, ag_recv.at[c, NEAR_ID[node]]).wait()
+        pass_on(c, 0, node)
+        pass_on(c, 1, node)
+
+    def from_far(c, half, node):
+        wait_far(c, half, node)
+        pass_on(c, half, node)
 
     def unfold(c):
         pltpu.make_async_copy(z_in.at[c], z_in.at[c], z_recv.at[c]).wait()
@@ -259,28 +255,62 @@
 
     nt = (((1,), (1,)), ((), ()))
 
-    def compute(c):
+    def fold_gain():
+        for copy in w_copies:
+            copy.wait()
+
+        @pl.loop(0, feat * mps // 128)
+        def _(i):
+            cols = pl.ds(pl.multiple_of(i * 128, 128), 128)
+            gain = gain_ref[pl.ds(i, 1), :]
+            for w in (gate_w, up_w):
+                w[:, cols] = (w[:, cols].astype(f32) * gain).astype(bf16)
+
+    def gate_up(c):
+        for half, node in FAR:
+            if not children(half, node):
+                wait_far(c, half, node)
         x = rows[c]
         gate = lax.dot_general(x, gate_w[...], nt, preferred_element_type=f32)
         up = lax.dot_general(x, up_w[...], nt, preferred_element_type=f32)
-        hidden[...] = (gate / (1.0 + jnp.exp(-gate)) * up).astype(bf16)
-
-        @pl.loop(0, mps * 2)
+        squares = jnp.zeros((segments * block, 128), f32)
+        for i in range(feat * mps // 128):
+            v = rows[c, :, i * 128 : (i + 1) * 128].astype(f32)
+            squares = squares + v * v
+        mean = jnp.sum(squares, axis=1, keepdims=True) / (feat * mps)
+        scale = lax.rsqrt(mean + EPSILON)
+        gate = gate * scale
+        hidden[c % 2] = (gate / (1.0 + jnp.exp(-gate)) * (up * scale)).astype(bf16)
+
+    def down(c, dy):
+        oy = lax.rem(mp + 2 * mps - sign(c) * dy, mps)
+
+        @pl.loop(0, 2)
         def _(i):
-            cols = pl.ds(pl.multiple_of(i * half_w, half_w), half_w)
+            cols = pl.ds(pl.multiple_of(oy * feat + i * half_w, half_w), half_w)
             parts[c, :, cols] = jnp.dot(
-                hidden[...], down_w[:, cols], preferred_element_type=f32
+                hidden[c % 2], down_w[:, cols], preferred_element_type=f32
             ).astype(bf16)
 
+        for half, node in FAR:
+            if node[1] == dy and not children(half, node):
+                send_far(c, half, node)
+
     def add_up(c, half, node):
-        r, f = spot(c, node, half)
-        acc = parts[c, r, f].astype(f32)
-        for n in children(half, node):
-            i = FAR_ID[half, n]
+        below = [FAR_ID[half, n] for n in children(half, node)]
+        for i in below:
             at = far_in.at[c, i]
             pltpu.make_async_copy(at, at, rs_recv.at[c, len(NEAR) + i]).wait()
-            acc = acc + far_in[c, i].astype(f32)
-        parts[c, r, f] = acc.astype(bf16)
+        ox, oy = origin(c, node)
+        f = pl.ds(pl.multiple_of(oy * feat + half * half_w, half_w), half_w)
+
+        @pl.loop(0, block // 16)
+        def _(k):
+            r = pl.ds(pl.multiple_of(ox * block + k * 16, 16), 16)
+            acc = parts[c, r, f].astype(f32)
+            for i in below:
+                acc = acc + far_in[c, i, pl.ds(pl.multiple_of(k * 16, 16), 16), :].astype(f32)
+            parts[c, r, f] = acc.astype(bf16)
 
     def send_far(c, half, node):
         r, f = spot(c, node, half)
@@ -294,27 +324,23 @@
             device_id_type=MESH_IDS,
         ).start()
 
-    def sums_at(c, below):
-        for half, node in FAR:
-            if depth_below(half, node) == below:
-                if below:
-                    add_up(c, half, node)
-                send_far(c, half, node)
-
-    def sums_near(c):
-        for node in NEAR:
-            for half in (0, 1):
-                if children(half, node):
-                    add_up(c, half, node)
-            r, f = spot(c, node)
-            pltpu.make_async_remote_copy(
-                src_ref=parts.at[c, r, f],
-                dst_ref=near_in.at[c, NEAR_ID[node]],
-                send_sem=rs_send.at[c],
-                recv_sem=rs_recv.at[c, NEAR_ID[node]],
-                device_id=hop(c, (-node[0], -node[1])),
-                device_id_type=MESH_IDS,
-            ).start()
+    def sum_far(c, half, node):
+        add_up(c, half, node)
+        send_far(c, half, node)
+
+    def sum_near(c, node):
+        for half in (0, 1):
+            if children(half, node):
+                add_up(c, half, node)
+        r, f = spot(c, node)
+        pltpu.make_async_remote_copy(
+            src_ref=parts.at[c, r, f],
+            dst_ref=near_in.at[c, NEAR_ID[node]],
+            send_sem=rs_send.at[c],
+            recv_sem=rs_recv.at[c, NEAR_ID[node]],
+            device_id=hop(c, (-node[0], -node[1])),
+            device_id_type=MESH_IDS,
+        ).start()
 
     def finish(c):
         r, _ = spot(c, (0, 0))
@@ -349,57 +375,32 @@
                 low, got, preferred_element_type=f32
             )
 
-    dispatch(0)
-    dispatch(1)
-    unfold(0)
-
-    @pl.loop(2, chunks)
-    def _(c):
-        dispatch(c)
-
-    for copy in w_copies:
-        copy.wait()
-
-    @pl.loop(0, chunks + 3)
-    def _(t):
-        def stage(lag, act):
-            c = t - lag
-            pl.when(jnp.logical_and(c >= 0, c < chunks))(lambda: act(c))
-
-        @functools.partial(stage, 0)
-        def _(c):
-            wait_rows(c, 1)
-            send_rows(c, 1)
-
-        stage(2, sums_near)
-        stage(-1, lambda c: pl.when(c >= 1)(lambda: unfold(c)))
-
-        @functools.partial(stage, 1)
-        def _(c):
-            wait_rows(c, 4)
-            compute(c)
-            sums_at(c, 0)
-
-        @functools.partial(stage, 0)
-        def _(c):
-            wait_rows(c, 2)
-            send_rows(c, 2)
-
-        stage(2, finish)
-        stage(1, lambda c: sums_at(c, 1))
-
-        @functools.partial(stage, 0)
-        def _(c):
-            wait_rows(c, 3)
-            send_rows(c, 3)
-
-        stage(1, lambda c: sums_at(c, 2))
-        stage(3, combine)
+    def weigh():
+        total[...] = tokens_ref[...].astype(f32)
+        weight = jnp.where(first, gates_ref[0:1, :], 0.0) + jnp.where(second, gates_ref[1:2, :], 0.0)
+        chosen_w[...] = jnp.transpose(weight)
+        chosen_n[...] = jnp.transpose(count[...])
+
+    steps = {
+        "z": lambda c: z_go(z_out, z_in, z_send, z_recv, c),
+        "uf": unfold,
+        "fn": from_near,
+        "ff": from_far,
+        "fold": fold_gain,
+        "gu": gate_up,
+        "dn": down,
+        "rf": sum_far,
+        "rn": sum_near,
+        "fi": finish,
+        "co": combine,
+    }
+    for name, *at in ORDER:
+        if name == "fold":
+            weigh()
+        steps[name](*at)
 
     out_ref[...] = total[...].astype(bf16)
 
-    for copy in sq_copies:
-        copy.wait_send()
     sent = segments * mps - 1
     tall = sent * block // mps
 
@@ -435,7 +436,7 @@
             vmem((hid, width), bf16),
             vmem((hid, width), bf16),
             vmem((hid, width), bf16),
-            vmem((segments * block, hid), bf16),
+            vmem((2, segments * block, hid), bf16),
             vmem((chunks, segments * block, width), bf16),
             vmem((chunks, segments * block, width), bf16),
             vmem((chunks, len(FAR), block, feat // 2), bf16),
@@ -445,12 +446,9 @@
             vmem((chunks, slots, fold), bf16),
             vmem((chunks, slots, fold), bf16),
             vmem((slots, tok), f32),
-            vmem((slots, tok), f32),
             vmem((tok, slots), f32),
             vmem((tok, slots), f32),
             vmem((tok, feat), f32),
-            vmem((8, tok), f32),
-            vmem((mps - 1, 8, tok), f32),
             dma((3,)),
             dma((chunks, IDS)),
             dma((chunks, IDS)),
@@ -460,8 +458,6 @@
             dma((chunks,)),
             dma((chunks,)),
             dma((chunks,)),
-            dma((mps - 1,)),
-            dma((mps - 1,)),
         ],
         compiler_params=pltpu.CompilerParams(
             collective_id=0, has_side_effects=True, vmem_limit_bytes=60 * 1024 * 1024
@@ -476,7 +472,7 @@
         tokens[0],
         jnp.swapaxes(routes, 1, 2)[0],
         jnp.swapaxes(gate_weights, 1, 2)[0],
-        norm_gain.reshape(mps, FOLDS, fold),
+        norm_gain.reshape(-1, 128),
         jnp.swapaxes(gate_proj, 1, 2)[0],
         jnp.swapaxes(up_proj, 1, 2)[0],
         down_proj[0],

time: 166 us -> 138 us (0.83)
  Pallas kernels: 162 us -> 136 us
    pallas_call x1, Pallas kernels: 162 us -> 136 us  [body(): pl.pallas_call(functools.partial(kernel, dims), out_shape=jax.ShapeDtypeS...]
where the time goes in v2:
time: 138 us
  Pallas kernels  136 us (99%)
  local copies, waits for them, and re-layouts  1.67 us (1%)
    pallas_call x1, Pallas kernels, body(): pl.pallas_call(functools.partial(kernel, dims), out_shape=jax.ShapeDtypeS...  136 us

profile of v2, /device:TPU:1, one launch (start us, length us, event | category | flops | bytes accessed | tf_op | source)
XLA Modules:
  0.0 137.9 jit_solution(531010640445056359)
XLA Ops:
  0.0 136.3 %expert_block.1 = bf16[128,1024]{1,0:T(8,128)(2,1)} custom-call(bf16[128,1024]{1,0:T(8,128)(2,1)} %bitcast.20, s32[2,128]{1,0:T(2,128)} %bitcast.22, f32[2,128]{1,0:T(2,128)} %bitcast.23, f32[32,128]{1,0:T(8,128)} %bitcast.21, bf16[448,4096]{1,0:T(8,128)(2,1)} %bitcast.17, bf16[448,4096]{1,0:T(8,128)(2,1)} %bitcast.18, bf16[448,4096]{1,0:T(8,128)(2,1)} %bitcast.19), custom_call_target="tpu_custom_call" | custom-call | flops 14092861440 | bytes 11010048 | tf_op jit(solution)/shard_map/expert_block/pallas_call | solution.py:430
  136.3 1.7 %copy.9 = bf16[1,128,1024]{2,1,0:T(8,128)(2,1)} copy(bf16[1,128,1024]{2,1,0:T(8,128)(2,1)} %bitcast.16) | data formatting | bytes 524288

commit v3 on v2

--- a/solution.py
+++ b/solution.py
@@ -57,39 +57,44 @@
     return tuple({3: -1, -3: 1}.get(v, v) for v in d)
 
 
+EARLY = (2, 3, 4)
+LATE = (0, 1)
+SIDES = [(half, (0, d) if half else (d, 0)) for half in (0, 1) for d in (1, -1, 2)]
+SIDE_ID = {m: i for i, m in enumerate(SIDES)}
+
 ORDER = (
-    ("z", 0), ("z", 1), ("fold",), ("uf", 0), ("uf", 1), ("z", 2), ("z", 3), ("fn", 0, (0, 1)),
-    ("fn", 0, (0, -1)), ("fn", 0, (1, 0)), ("fn", 0, (-1, 0)), ("z", 4), ("fn", 1, (0, -1)), ("fn", 1, (0, 1)),
-    ("ff", 0, 1, (0, 2)), ("ff", 0, 1, (1, 1)), ("fn", 1, (1, 0)), ("ff", 0, 0, (1, 1)), ("ff", 0, 1, (-1, -1)),
-    ("fn", 1, (-1, 0)), ("ff", 0, 0, (-1, -1)), ("ff", 0, 0, (2, 0)), ("ff", 1, 1, (0, 2)),
-    ("ff", 1, 1, (-1, -1)), ("ff", 1, 0, (1, 1)), ("ff", 1, 1, (1, 1)), ("uf", 2), ("ff", 0, 1, (1, 2)),
-    ("ff", 1, 0, (-1, -1)), ("ff", 1, 0, (2, 0)), ("ff", 0, 0, (2, 1)), ("uf", 3), ("ff", 1, 1, (1, 2)),
-    ("uf", 4), ("fn", 2, (0, 1)), ("fn", 2, (0, -1)), ("ff", 1, 0, (2, 1)), ("fn", 2, (1, 0)),
-    ("fn", 2, (-1, 0)), ("gu", 0), ("dn", 0, 2), ("dn", 0, 1), ("dn", 0, -1), ("dn", 0, 0),
-    ("ff", 2, 1, (0, 2)), ("ff", 2, 1, (1, 1)), ("fn", 3, (0, 1)), ("ff", 2, 0, (1, 1)), ("ff", 2, 1, (-1, -1)),
-    ("fn", 3, (0, -1)), ("ff", 2, 0, (-1, -1)), ("ff", 2, 0, (2, 0)), ("fn", 3, (1, 0)), ("fn", 3, (-1, 0)),
-    ("gu", 1), ("dn", 1, 2), ("dn", 1, 1), ("dn", 1, -1), ("dn", 1, 0), ("ff", 3, 1, (0, 2)),
-    ("ff", 3, 1, (1, 1)), ("ff", 2, 1, (1, 2)), ("rf", 0, 1, (1, 2)), ("rf", 0, 0, (1, 1)),
-    ("rf", 0, 1, (1, 1)), ("rf", 0, 0, (2, 1)), ("rf", 0, 0, (-1, -1)), ("rf", 0, 1, (-1, -1)),
-    ("ff", 3, 0, (1, 1)), ("ff", 2, 0, (2, 1)), ("fn", 4, (0, 1)), ("ff", 3, 1, (-1, -1)), ("ff", 3, 0, (2, 0)),
-    ("ff", 3, 0, (-1, -1)), ("fn", 4, (0, -1)), ("fn", 4, (1, 0)), ("fn", 4, (-1, 0)), ("rf", 1, 0, (1, 1)),
-    ("rf", 1, 1, (1, 2)), ("rf", 1, 0, (-1, -1)), ("rf", 1, 0, (2, 1)), ("rf", 1, 1, (1, 1)),
-    ("rf", 1, 1, (-1, -1)), ("ff", 3, 1, (1, 2)), ("rn", 0, (-1, 0)), ("rf", 0, 0, (2, 0)),
-    ("ff", 4, 1, (0, 2)), ("rf", 0, 1, (0, 2)), ("rn", 0, (0, -1)), ("ff", 4, 1, (1, 1)), ("ff", 3, 0, (2, 1)),
-    ("gu", 2), ("dn", 2, 2), ("dn", 2, 1), ("dn", 2, -1), ("dn", 2, 0), ("ff", 4, 0, (1, 1)),
-    ("ff", 4, 0, (-1, -1)), ("ff", 4, 1, (-1, -1)), ("ff", 4, 0, (2, 0)), ("rf", 1, 1, (0, 2)),
-    ("rf", 1, 0, (2, 0)), ("rn", 0, (0, 1)), ("rn", 0, (1, 0)), ("rn", 1, (0, -1)), ("rf", 2, 0, (1, 1)),
-    ("rn", 1, (-1, 0)), ("ff", 4, 1, (1, 2)), ("rf", 2, 1, (1, 2)), ("rf", 2, 0, (2, 1)), ("gu", 3),
-    ("dn", 3, 2), ("dn", 3, 1), ("dn", 3, -1), ("dn", 3, 0), ("ff", 4, 0, (2, 1)), ("rf", 2, 1, (1, 1)),
-    ("rf", 2, 0, (-1, -1)), ("rf", 2, 1, (-1, -1)), ("fi", 0), ("rf", 3, 0, (1, 1)), ("rn", 1, (0, 1)),
-    ("rn", 1, (1, 0)), ("rf", 2, 1, (0, 2)), ("rf", 3, 1, (1, 2)), ("rf", 3, 0, (2, 1)), ("rf", 2, 0, (2, 0)),
-    ("rf", 3, 1, (1, 1)), ("gu", 4), ("dn", 4, 2), ("dn", 4, 1), ("dn", 4, -1), ("dn", 4, 0),
-    ("rf", 3, 1, (0, 2)), ("rf", 3, 0, (-1, -1)), ("rf", 3, 1, (-1, -1)), ("rf", 3, 0, (2, 0)), ("fi", 1),
-    ("rf", 4, 1, (1, 2)), ("rf", 4, 0, (1, 1)), ("rf", 4, 1, (1, 1)), ("rf", 4, 0, (2, 1)),
-    ("rf", 4, 0, (-1, -1)), ("rn", 2, (0, 1)), ("rf", 4, 1, (-1, -1)), ("rn", 2, (0, -1)), ("rn", 2, (1, 0)),
-    ("rf", 4, 1, (0, 2)), ("rn", 2, (-1, 0)), ("rf", 4, 0, (2, 0)), ("rn", 3, (0, 1)), ("rn", 3, (0, -1)),
-    ("rn", 3, (1, 0)), ("rn", 3, (-1, 0)), ("rn", 4, (0, -1)), ("rn", 4, (-1, 0)), ("fi", 2), ("rn", 4, (0, 1)),
-    ("rn", 4, (1, 0)), ("fi", 3), ("fi", 4), ("co", 0), ("co", 1), ("co", 2), ("co", 3), ("co", 4),
+    ("mq", 2), ("mq", 3), ("mq", 4), ("z", 0), ("fold",), ("uf", 0), ("z", 1), ("mf", 2), ("z", 2), ("mf", 3),
+    ("z", 3), ("mf", 4), ("fn", 0, (0, 1)), ("fn", 0, (0, -1)), ("fn", 0, (1, 0)), ("fn", 0, (-1, 0)), ("z", 4),
+    ("uf", 1), ("zx", 2), ("ff", 0, 1, (0, 2)), ("ff", 0, 1, (1, 1)), ("ff", 0, 1, (-1, -1)), ("uf", 2),
+    ("ff", 0, 0, (1, 1)), ("ff", 0, 0, (-1, -1)), ("zx", 3), ("ff", 0, 0, (2, 0)), ("uf", 3), ("fn", 1, (0, 1)),
+    ("fn", 1, (1, 0)), ("zx", 4), ("fn", 1, (0, -1)), ("fn", 1, (-1, 0)), ("uf", 4), ("fn", 2, (0, 1)),
+    ("fn", 2, (0, -1)), ("ff", 0, 1, (1, 2)), ("fn", 2, (-1, 0)), ("ff", 0, 0, (2, 1)), ("fn", 3, (0, 1)),
+    ("fn", 2, (1, 0)), ("fn", 3, (1, 0)), ("fn", 3, (0, -1)), ("fn", 3, (-1, 0)), ("ff", 1, 1, (0, 2)),
+    ("ff", 1, 1, (1, 1)), ("ff", 1, 0, (1, 1)), ("ff", 1, 0, (2, 0)), ("ff", 1, 1, (-1, -1)), ("ux", 2),
+    ("fn", 4, (0, -1)), ("fn", 4, (0, 1)), ("fn", 4, (-1, 0)), ("fn", 4, (1, 0)), ("ff", 1, 0, (-1, -1)),
+    ("gu", 0), ("ff", 1, 1, (1, 2)), ("ff", 1, 0, (2, 1)), ("dn", 0, 2), ("dn", 0, 1), ("dn", 0, -1),
+    ("dn", 0, 0), ("ff", 2, 0, (1, 1)), ("ff", 2, 1, (1, 1)), ("ff", 2, 0, (-1, -1)), ("ff", 2, 1, (-1, -1)),
+    ("rn", 0, (0, 1)), ("ff", 2, 0, (2, 1)), ("rn", 0, (1, 0)), ("ux", 3), ("ff", 2, 1, (1, 2)), ("gu", 1),
+    ("rf", 0, 1, (1, 2)), ("rf", 0, 0, (1, 1)), ("rf", 0, 1, (1, 1)), ("rf", 0, 0, (2, 1)),
+    ("rf", 0, 0, (-1, -1)), ("rf", 0, 1, (-1, -1)), ("dn", 1, 2), ("dn", 1, 1), ("dn", 1, -1), ("dn", 1, 0),
+    ("ff", 3, 0, (1, 1)), ("ff", 3, 1, (1, 1)), ("rn", 0, (0, -1)), ("rn", 0, (-1, 0)), ("rn", 1, (0, 1)),
+    ("rn", 1, (1, 0)), ("ux", 4), ("ff", 3, 1, (1, 2)), ("ff", 3, 0, (2, 1)), ("ff", 3, 0, (-1, -1)),
+    ("ff", 3, 1, (-1, -1)), ("gu", 2), ("fs", 0), ("rf", 1, 1, (1, 2)), ("rf", 1, 0, (1, 1)),
+    ("rf", 1, 1, (1, 1)), ("rf", 1, 0, (2, 1)), ("rf", 1, 0, (-1, -1)), ("rf", 1, 1, (-1, -1)), ("dn", 2, 2),
+    ("dn", 2, 1), ("dn", 2, -1), ("dn", 2, 0), ("ff", 4, 0, (1, 1)), ("ff", 4, 1, (1, 1)), ("fi", 0),
+    ("ff", 4, 1, (1, 2)), ("ff", 4, 0, (2, 1)), ("ff", 4, 0, (-1, -1)), ("ff", 4, 1, (-1, -1)),
+    ("rn", 1, (0, -1)), ("rn", 1, (-1, 0)), ("gu", 3), ("fs", 1), ("rf", 2, 1, (1, 2)), ("rf", 2, 0, (1, 1)),
+    ("rf", 2, 1, (1, 1)), ("rf", 2, 0, (2, 1)), ("rf", 2, 0, (-1, -1)), ("rf", 2, 1, (-1, -1)), ("dn", 3, 2),
+    ("dn", 3, 1), ("dn", 3, -1), ("rf", 2, 1, (0, 2)), ("dn", 3, 0), ("rf", 2, 0, (2, 0)), ("gu", 4),
+    ("rf", 3, 1, (1, 2)), ("rf", 3, 0, (1, 1)), ("rf", 3, 1, (1, 1)), ("rf", 3, 0, (2, 1)),
+    ("rf", 3, 0, (-1, -1)), ("rf", 3, 1, (-1, -1)), ("dn", 4, 2), ("dn", 4, 1), ("rf", 3, 1, (0, 2)),
+    ("dn", 4, -1), ("dn", 4, 0), ("rf", 3, 0, (2, 0)), ("fi", 1), ("rf", 4, 1, (1, 2)), ("rf", 4, 0, (1, 1)),
+    ("rf", 4, 1, (1, 1)), ("rf", 4, 0, (2, 1)), ("rf", 4, 0, (-1, -1)), ("rf", 4, 1, (-1, -1)),
+    ("rn", 2, (0, 1)), ("rn", 2, (0, -1)), ("rf", 4, 1, (0, 2)), ("rn", 2, (1, 0)), ("rn", 2, (-1, 0)),
+    ("rf", 4, 0, (2, 0)), ("rn", 3, (0, 1)), ("rn", 3, (0, -1)), ("rn", 3, (1, 0)), ("rn", 3, (-1, 0)),
+    ("l1", 0), ("rn", 4, (0, -1)), ("rn", 4, (-1, 0)), ("fi", 2), ("rn", 4, (0, 1)), ("rn", 4, (1, 0)),
+    ("fi", 3), ("l2", 0), ("l1", 1), ("fi", 4), ("l2", 1), ("co", 0), ("co", 2), ("co", 3), ("co", 1),
+    ("co", 4),
 )
 
 
@@ -98,13 +103,15 @@
     tokens_ref, routes_ref, gates_ref, gain_ref, gate_hbm, up_hbm, down_hbm,
     out_ref,
     gate_w, up_w, down_w, hidden, rows, parts, far_in, near_in,
-    z_out, z_in, b_out, b_in, count, chosen_w, chosen_n, total,
+    z_out, z_in, b_out, b_in, side, side_in, late_out, late_in, late_near, count, chosen_w, chosen_n, total,
     w_sem, ag_recv, rs_recv, ag_send, rs_send, z_send, z_recv, b_send, b_recv,
+    side_send, side_recv, x_send, x_recv, y_send, y_recv, late_send, late_recv,
 ):
     experts, segments, mps, tok, feat, chunks = dims
     f32, bf16 = jnp.float32, jnp.bfloat16
     fold = feat // FOLDS
     half_w = feat // 2
+    part = half_w // FOLDS
     per = FOLDS * SLOTS
     slots = experts * per
     block = experts * SLOTS
@@ -154,26 +161,32 @@
         for g in range(FOLDS):
             pick = jnp.where(row_fold == g, fill, 0.0).astype(bf16)
             picked = picked + jnp.dot(
-                pick, tokens_ref[:, g * fold : (g + 1) * fold], preferred_element_type=f32
+                pick,
+                jnp.concatenate(
+                    [tokens_ref[:, h * half_w + g * part : h * half_w + (g + 1) * part] for h in (0, 1)],
+                    axis=1,
+                ),
+                preferred_element_type=f32,
             )
         z_out[c] = picked.astype(bf16)
 
     pl.semaphore_wait(barrier, experts - 1 + 4)
 
-    def z_go(out, got, send, recv, c):
+    def z_go(out, got, send, recv, c, i=None):
+        i = c if i is None else i
         base = pl.multiple_of(exp * per, per)
         pltpu.make_async_copy(
-            out.at[c, pl.ds(base, per), :], got.at[c, pl.ds(base, per), :], recv.at[c]
+            out.at[i, pl.ds(base, per), :], got.at[i, pl.ds(base, per), :], recv.at[i]
         ).start()
 
         @pl.loop(1, experts)
         def _(d):
             other = lax.rem(exp + d, experts)
             pltpu.make_async_remote_copy(
-                src_ref=out.at[c, pl.ds(pl.multiple_of(other * per, per), per), :],
-                dst_ref=got.at[c, pl.ds(base, per), :],
-                send_sem=send.at[c],
-                recv_sem=recv.at[c],
+                src_ref=out.at[i, pl.ds(pl.multiple_of(other * per, per), per), :],
+                dst_ref=got.at[i, pl.ds(base, per), :],
+                send_sem=send.at[i],
+                recv_sem=recv.at[i],
                 device_id={"expert": other},
                 device_id_type=MESH_IDS,
             ).start()
@@ -200,9 +213,14 @@
             return {"segment": lax.rem(seg + segments + s * move[0], segments)}
         return {"mp": lax.rem(mp + mps + s * move[1], mps)}
 
+    def near_half(c, node):
+        if c in EARLY:
+            return 1 if node[0] else 0
+        return None
+
     def send_near(c):
-        r, f = spot(c, (0, 0))
         for node in NEAR:
+            r, f = spot(c, (0, 0), near_half(c, node))
             pltpu.make_async_remote_copy(
                 src_ref=rows.at[c, r, f],
                 dst_ref=rows.at[c, r, f],
@@ -214,6 +232,8 @@
 
     def pass_on(c, half, node):
         for n in children(half, node):
+            if c in EARLY and (half, n) in SIDE_ID:
+                continue
             r, f = spot(c, node, half)
             pltpu.make_async_remote_copy(
                 src_ref=rows.at[c, r, f],
@@ -230,11 +250,12 @@
         pltpu.make_async_copy(at, at, ag_recv.at[c, len(NEAR) + FAR_ID[half, node]]).wait()
 
     def from_near(c, node):
-        r, f = spot(c, node)
+        only = near_half(c, node)
+        r, f = spot(c, node, only)
         at = rows.at[c, r, f]
         pltpu.make_async_copy(at, at, ag_recv.at[c, NEAR_ID[node]]).wait()
-        pass_on(c, 0, node)
-        pass_on(c, 1, node)
+        for half in (0, 1) if only is None else (only,):
+            pass_on(c, half, node)
 
     def from_far(c, half, node):
         wait_far(c, half, node)
@@ -242,16 +263,65 @@
 
     def unfold(c):
         pltpu.make_async_copy(z_in.at[c], z_in.at[c], z_recv.at[c]).wait()
-        got = z_in[c]
+        spread(c, z_in[c], [(0, (0, 0)), (1, (0, 0))])
+        send_near(c)
+
+    def spread(c, got, places):
         r_, q_ = iota((block, slots), 0), iota((block, slots), 1)
         place = (r_ // SLOTS) * per + lax.rem(r_, SLOTS)
-        ox = pl.multiple_of(seg * block, block)
         for g in range(FOLDS):
             pick = jnp.where(q_ == place + g * SLOTS, 1.0, 0.0).astype(bf16)
-            rows[c, pl.ds(ox, block), pl.ds(pl.multiple_of(mp * feat + g * fold, fold), fold)] = (
-                jnp.dot(pick, got, preferred_element_type=f32).astype(bf16)
-            )
-        send_near(c)
+            whole = jnp.dot(pick, got, preferred_element_type=f32).astype(bf16)
+            for i, (half, node) in enumerate(places):
+                ox, oy = origin(c, node)
+                rows[
+                    c,
+                    pl.ds(pl.multiple_of(ox * block, block), block),
+                    pl.ds(pl.multiple_of(oy * feat + half * half_w + g * part, part), part),
+                ] = whole[:, i * part : (i + 1) * part]
+
+    def side_copy(c, half, node, own):
+        e, i = EARLY.index(c), SIDE_ID[half, node]
+        up = (0, 0) if own else parent(half, node)
+        lane = lambda k: pl.ds(k * part, part)
+        src = z_out.at[c, :, lane(half)] if own else side.at[e, :, lane(SIDE_ID[half, up])]
+        return pltpu.make_async_remote_copy(
+            src_ref=src,
+            dst_ref=side.at[e, :, lane(i)],
+            send_sem=side_send.at[e],
+            recv_sem=side_recv.at[e, i],
+            device_id=hop(c, step_of(up, node)),
+            device_id_type=MESH_IDS,
+        )
+
+    def side_wait(c, half, node):
+        e, i = EARLY.index(c), SIDE_ID[half, node]
+        at = side.at[e, :, pl.ds(i * part, part)]
+        pltpu.make_async_copy(at, at, side_recv.at[e, i]).wait()
+
+    def side_first(c):
+        for half, node in SIDES:
+            if level(node) == 1:
+                side_copy(c, half, node, True).start()
+
+    def side_next(c):
+        for half, node in SIDES:
+            if level(node) == 2:
+                side_wait(c, half, parent(half, node))
+                side_copy(c, half, node, False).start()
+
+    def side_out(c):
+        for half, node in SIDES:
+            if level(node) == 2 or node not in [parent(h, n) for h, n in SIDES if h == half]:
+                side_wait(c, half, node)
+        z_go(side, side_in, x_send, x_recv, c, EARLY.index(c))
+
+    def side_unfold(c):
+        e = EARLY.index(c)
+        pltpu.make_async_copy(side_in.at[e], side_in.at[e], x_recv.at[e]).wait()
+        spread(c, side_in[e], SIDES)
+        for half, node in SIDES:
+            pass_on(c, half, node)
 
     nt = (((1,), (1,)), ((), ()))
 
@@ -297,7 +367,7 @@
                 send_far(c, half, node)
 
     def add_up(c, half, node):
-        below = [FAR_ID[half, n] for n in children(half, node)]
+        below = [FAR_ID[half, n] for n in children(half, node) if not (c in LATE and (half, n) in SIDE_ID)]
         for i in below:
             at = far_in.at[c, i]
             pltpu.make_async_copy(at, at, rs_recv.at[c, len(NEAR) + i]).wait()
@@ -329,35 +399,114 @@
         send_far(c, half, node)
 
     def sum_near(c, node):
-        for half in (0, 1):
+        only = (1 if node[0] else 0) if c in LATE else None
+        for half in (0, 1) if only is None else (only,):
             if children(half, node):
                 add_up(c, half, node)
-        r, f = spot(c, node)
+        r, f = spot(c, node, only)
+        at = near_in.at[c, NEAR_ID[node]]
+        if only is not None:
+            at = near_in.at[c, NEAR_ID[node], :, pl.ds(only * half_w, half_w)]
         pltpu.make_async_remote_copy(
             src_ref=parts.at[c, r, f],
-            dst_ref=near_in.at[c, NEAR_ID[node]],
+            dst_ref=at,
             send_sem=rs_send.at[c],
             recv_sem=rs_recv.at[c, NEAR_ID[node]],
             device_id=hop(c, (-node[0], -node[1])),
             device_id_type=MESH_IDS,
         ).start()
 
-    def finish(c):
-        r, _ = spot(c, (0, 0))
-        for i in range(len(NEAR)):
-            at = near_in.at[c, i]
-            pltpu.make_async_copy(at, at, rs_recv.at[c, i]).wait()
+    def gather_up(pieces):
         q_, r_ = iota((slots, block), 0), iota((slots, block), 1)
         place = (r_ // SLOTS) * per + lax.rem(r_, SLOTS)
-        back = jnp.zeros((slots, fold), f32)
+        back = None
         for g in range(FOLDS):
-            acc = parts[c, r, pl.ds(pl.multiple_of(mp * feat + g * fold, fold), fold)].astype(f32)
-            for i in range(len(NEAR)):
-                acc = acc + near_in[c, i, :, g * fold : (g + 1) * fold].astype(f32)
             pick = jnp.where(q_ == place + g * SLOTS, 1.0, 0.0).astype(bf16)
-            back = back + jnp.dot(pick, acc.astype(bf16), preferred_element_type=f32)
-        b_out[c] = back.astype(bf16)
+            add = jnp.dot(pick, pieces(g), preferred_element_type=f32)
+            back = add if back is None else back + add
+        return back.astype(bf16)
+
+    def finish(c):
+        late = c in LATE
+        for node in NEAR:
+            i = NEAR_ID[node]
+            at = near_in.at[c, i]
+            if late:
+                at = near_in.at[c, i, :, pl.ds((1 if node[0] else 0) * half_w, half_w)]
+            pltpu.make_async_copy(at, at, rs_recv.at[c, i]).wait()
+        ox = pl.ds(pl.multiple_of(seg * block, block), block)
+
+        def pieces(g):
+            both = []
+            for half in (0, 1):
+                at = half * half_w + g * part
+                acc = parts[c, ox, pl.ds(pl.multiple_of(mp * feat + at, part), part)].astype(f32)
+                for node in NEAR:
+                    if not late or half == (1 if node[0] else 0):
+                        acc = acc + near_in[c, NEAR_ID[node], :, at : at + part].astype(f32)
+                both.append(acc.astype(bf16))
+            return jnp.concatenate(both, axis=1)
+
+        b_out[c] = gather_up(pieces)
         z_go(b_out, b_in, b_send, b_recv, c)
+
+    def finish_side(c):
+        e = LATE.index(c)
+        for half, node in SIDES:
+            add_up(c, half, node)
+
+        def pieces(g):
+            whole = []
+            for half, node in SIDES:
+                ox, oy = origin(c, node)
+                whole.append(
+                    parts[
+                        c,
+                        pl.ds(pl.multiple_of(ox * block, block), block),
+                        pl.ds(pl.multiple_of(oy * feat + half * half_w + g * part, part), part),
+                    ]
+                )
+            return jnp.concatenate(whole, axis=1)
+
+        late_out[e] = gather_up(pieces)
+        z_go(late_out, late_in, y_send, y_recv, c, e)
+
+    def late_copy(c, half, node):
+        e, i = LATE.index(c), SIDE_ID[half, node]
+        up = parent(half, node)
+        return pltpu.make_async_remote_copy(
+            src_ref=late_in.at[e, :, pl.ds(i * part, part)],
+            dst_ref=late_near.at[e, :, pl.ds(i * part, part)],
+            send_sem=late_send.at[e],
+            recv_sem=late_recv.at[e, i],
+            device_id=hop(c, step_of(node, up)),
+            device_id_type=MESH_IDS,
+        )
+
+    def late_wait(c, half, node):
+        e, i = LATE.index(c), SIDE_ID[half, node]
+        at = late_near.at[e, :, pl.ds(i * part, part)]
+        pltpu.make_async_copy(at, at, late_recv.at[e, i]).wait()
+
+    def late_first(c):
+        e = LATE.index(c)
+        pltpu.make_async_copy(late_in.at[e], late_in.at[e], y_recv.at[e]).wait()
+        inner = [(h, parent(h, n)) for h, n in SIDES if level(n) == 2]
+        for half, node in SIDES:
+            if (half, node) not in inner:
+                late_copy(c, half, node).start()
+
+    def late_next(c):
+        e = LATE.index(c)
+        for half, node in SIDES:
+            if level(node) == 2:
+                late_wait(c, half, node)
+                up = parent(half, node)
+                f, n = (slice(SIDE_ID[half, v] * part, (SIDE_ID[half, v] + 1) * part) for v in (node, up))
+                late_in[e, :, n] = (
+                    late_in[e, :, n].astype(f32) + late_near[e, :, f].astype(f32)
+                ).astype(bf16)
+                late_copy(c, half, up).start()
 
     lane_fold = lax.rem(iota((tok, slots), 1), per) // SLOTS
     lane_slot = lax.rem(iota((tok, slots), 1), SLOTS)
@@ -365,15 +514,29 @@
     def combine(c):
         pltpu.make_async_copy(b_in.at[c], b_in.at[c], b_recv.at[c]).wait()
         got = b_in[c]
+        if c in LATE:
+            e = LATE.index(c)
+            lanes = []
+            for half in (0, 1):
+                acc = got[:, half * part : (half + 1) * part].astype(f32)
+                for h, node in SIDES:
+                    if h == half and level(node) == 1:
+                        late_wait(c, half, node)
+                        i = SIDE_ID[half, node]
+                        acc = acc + late_near[e, :, i * part : (i + 1) * part].astype(f32)
+                lanes.append(acc.astype(bf16))
+            got = jnp.concatenate(lanes, axis=1)
         share = jnp.where(chosen_n[...] == (lane_slot + SLOTS * c).astype(f32), chosen_w[...], 0.0)
         for g in range(FOLDS):
-            part = jnp.where(lane_fold == g, share, 0.0)
-            high = part.astype(bf16)
-            low = (part - high.astype(f32)).astype(bf16)
-            cols = slice(g * fold, (g + 1) * fold)
-            total[:, cols] += jnp.dot(high, got, preferred_element_type=f32) + jnp.dot(
+            mine = jnp.where(lane_fold == g, share, 0.0)
+            high = mine.astype(bf16)
+            low = (mine - high.astype(f32)).astype(bf16)
+            add = jnp.dot(high, got, preferred_element_type=f32) + jnp.dot(
                 low, got, preferred_element_type=f32
             )
+            for half in (0, 1):
+                at = half * half_w + g * part
+                total[:, at : at + part] += add[:, half * part : (half + 1) * part]
 
     def weigh():
         total[...] = tokens_ref[...].astype(f32)
@@ -383,7 +546,11 @@
 
     steps = {
         "z": lambda c: z_go(z_out, z_in, z_send, z_recv, c),
+        "mq": side_first,
+        "mf": side_next,
+        "zx": side_out,
         "uf": unfold,
+        "ux": side_unfold,
         "fn": from_near,
         "ff": from_far,
         "fold": fold_gain,
@@ -392,6 +559,9 @@
         "rf": sum_far,
         "rn": sum_near,
         "fi": finish,
+        "fs": finish_side,
+        "l1": late_first,
+        "l2": late_next,
         "co": combine,
     }
     for name, *at in ORDER:
@@ -401,17 +571,29 @@
 
     out_ref[...] = total[...].astype(bf16)
 
-    sent = segments * mps - 1
-    tall = sent * block // mps
-
-    @pl.loop(0, chunks)
-    def _(c):
-        for ref, sem in ((rows, ag_send), (parts, rs_send)):
-            at = ref.at[c, 0:tall, :]
+    def blocks(chunk_list, count, ref, sem):
+        for c in chunk_list:
+            at = ref.at[c, 0 : count * block // (2 * mps), :]
             pltpu.make_async_copy(at, at, sem.at[c]).wait()
-        for ref, sem in ((z_out, z_send), (b_out, b_send)):
+
+    whole = 2 * (segments * mps - 1)
+    short = len(SIDES)
+    blocks([c for c in range(chunks) if c not in EARLY], whole, rows, ag_send)
+    blocks(EARLY, whole - short, rows, ag_send)
+    blocks([c for c in range(chunks) if c not in LATE], whole, parts, rs_send)
+    blocks(LATE, whole - short, parts, rs_send)
+    for ref, sem, n in (
+        (z_out, z_send, chunks),
+        (b_out, b_send, chunks),
+        (side, x_send, len(EARLY)),
+        (late_out, y_send, len(LATE)),
+    ):
+        for c in range(n):
             at = ref.at[c, 0 : slots - per, :]
             pltpu.make_async_copy(at, at, sem.at[c]).wait()
+    for ref, sem, n in ((side, side_send, len(EARLY)), (late_in, late_send, len(LATE))):
+        for c in range(n):
+            pltpu.make_async_copy(ref.at[c], ref.at[c], sem.at[c]).wait()
 
 
 def body(tokens, routes, gate_weights, norm_gain, gate_proj, up_proj, down_proj):
@@ -426,6 +608,7 @@
     width = feat * mps
     dims = (experts, segments, mps, tok, feat, chunks)
     bf16, f32 = jnp.bfloat16, jnp.float32
+    early, late = max(len(EARLY), 1), max(len(LATE), 1)
     vmem, dma = pltpu.VMEM, pltpu.SemaphoreType.DMA
     out = pl.pallas_call(
         functools.partial(kernel, dims),
@@ -445,6 +628,11 @@
             vmem((chunks, slots, fold), bf16),
             vmem((chunks, slots, fold), bf16),
             vmem((chunks, slots, fold), bf16),
+            vmem((early, slots, len(SIDES) * fold // 2), bf16),
+            vmem((early, slots, len(SIDES) * fold // 2), bf16),
+            vmem((late, slots, len(SIDES) * fold // 2), bf16),
+            vmem((late, slots, len(SIDES) * fold // 2), bf16),
+            vmem((late, slots, len(SIDES) * fold // 2), bf16),
             vmem((slots, tok), f32),
             vmem((tok, slots), f32),
             vmem((tok, slots), f32),
@@ -458,6 +646,14 @@
             dma((chunks,)),
             dma((chunks,)),
             dma((chunks,)),
+            dma((early,)),
+            dma((early, len(SIDES))),
+            dma((early,)),
+            dma((early,)),
+            dma((late,)),
+            dma((late,)),
+            dma((late,)),
+            dma((late, len(SIDES))),
         ],
         compiler_params=pltpu.CompilerParams(
             collective_id=0, has_side_effects=True, vmem_limit_bytes=60 * 1024 * 1024

time: 138 us -> 133 us (0.964)
  Pallas kernels: 136 us -> 131 us
    pallas_call x1, Pallas kernels: 136 us -> 131 us  [body(): pl.pallas_call(functools.partial(kernel, dims), out_shape=jax.ShapeDtypeS...]
where the time goes in v3:
time: 133 us
  Pallas kernels  131 us (98%)
  local copies, waits for them, and re-layouts  1.67 us (1%)
    pallas_call x1, Pallas kernels, body(): pl.pallas_call(functools.partial(kernel, dims), out_shape=jax.ShapeDtypeS...  131 us

profile of v3, /device:TPU:1, one launch (start us, length us, event | category | flops | bytes accessed | tf_op | source)
XLA Modules:
  0.0 132.9 jit_solution(8901660825912467999)
XLA Ops:
  0.0 131.2 %expert_block.1 = bf16[128,1024]{1,0:T(8,128)(2,1)} custom-call(bf16[128,1024]{1,0:T(8,128)(2,1)} %bitcast.20, s32[2,128]{1,0:T(2,128)} %bitcast.22, f32[2,128]{1,0:T(2,128)} %bitcast.23, f32[32,128]{1,0:T(8,128)} %bitcast.21, bf16[448,4096]{1,0:T(8,128)(2,1)} %bitcast.17, bf16[448,4096]{1,0:T(8,128)(2,1)} %bitcast.18, bf16[448,4096]{1,0:T(8,128)(2,1)} %bitcast.19), custom_call_target="tpu_custom_call" | custom-call | flops 14092861440 | bytes 11010048 | tf_op jit(solution)/shard_map/expert_block/pallas_call | solution.py:613
  131.2 1.7 %copy.9 = bf16[1,128,1024]{2,1,0:T(8,128)(2,1)} copy(bf16[1,128,1024]{2,1,0:T(8,128)(2,1)} %bitcast.16) | data formatting | bytes 524288

commit v4 on v3

--- a/solution.py
+++ b/solution.py
@@ -58,43 +58,43 @@
 
 
 EARLY = (2, 3, 4)
-LATE = (0, 1)
+LATE = (0, 1, 2)
 SIDES = [(half, (0, d) if half else (d, 0)) for half in (0, 1) for d in (1, -1, 2)]
 SIDE_ID = {m: i for i, m in enumerate(SIDES)}
 
 ORDER = (
-    ("mq", 2), ("mq", 3), ("mq", 4), ("z", 0), ("fold",), ("uf", 0), ("z", 1), ("mf", 2), ("z", 2), ("mf", 3),
-    ("z", 3), ("mf", 4), ("fn", 0, (0, 1)), ("fn", 0, (0, -1)), ("fn", 0, (1, 0)), ("fn", 0, (-1, 0)), ("z", 4),
-    ("uf", 1), ("zx", 2), ("ff", 0, 1, (0, 2)), ("ff", 0, 1, (1, 1)), ("ff", 0, 1, (-1, -1)), ("uf", 2),
-    ("ff", 0, 0, (1, 1)), ("ff", 0, 0, (-1, -1)), ("zx", 3), ("ff", 0, 0, (2, 0)), ("uf", 3), ("fn", 1, (0, 1)),
-    ("fn", 1, (1, 0)), ("zx", 4), ("fn", 1, (0, -1)), ("fn", 1, (-1, 0)), ("uf", 4), ("fn", 2, (0, 1)),
-    ("fn", 2, (0, -1)), ("ff", 0, 1, (1, 2)), ("fn", 2, (-1, 0)), ("ff", 0, 0, (2, 1)), ("fn", 3, (0, 1)),
-    ("fn", 2, (1, 0)), ("fn", 3, (1, 0)), ("fn", 3, (0, -1)), ("fn", 3, (-1, 0)), ("ff", 1, 1, (0, 2)),
-    ("ff", 1, 1, (1, 1)), ("ff", 1, 0, (1, 1)), ("ff", 1, 0, (2, 0)), ("ff", 1, 1, (-1, -1)), ("ux", 2),
-    ("fn", 4, (0, -1)), ("fn", 4, (0, 1)), ("fn", 4, (-1, 0)), ("fn", 4, (1, 0)), ("ff", 1, 0, (-1, -1)),
-    ("gu", 0), ("ff", 1, 1, (1, 2)), ("ff", 1, 0, (2, 1)), ("dn", 0, 2), ("dn", 0, 1), ("dn", 0, -1),
-    ("dn", 0, 0), ("ff", 2, 0, (1, 1)), ("ff", 2, 1, (1, 1)), ("ff", 2, 0, (-1, -1)), ("ff", 2, 1, (-1, -1)),
-    ("rn", 0, (0, 1)), ("ff", 2, 0, (2, 1)), ("rn", 0, (1, 0)), ("ux", 3), ("ff", 2, 1, (1, 2)), ("gu", 1),
-    ("rf", 0, 1, (1, 2)), ("rf", 0, 0, (1, 1)), ("rf", 0, 1, (1, 1)), ("rf", 0, 0, (2, 1)),
-    ("rf", 0, 0, (-1, -1)), ("rf", 0, 1, (-1, -1)), ("dn", 1, 2), ("dn", 1, 1), ("dn", 1, -1), ("dn", 1, 0),
-    ("ff", 3, 0, (1, 1)), ("ff", 3, 1, (1, 1)), ("rn", 0, (0, -1)), ("rn", 0, (-1, 0)), ("rn", 1, (0, 1)),
-    ("rn", 1, (1, 0)), ("ux", 4), ("ff", 3, 1, (1, 2)), ("ff", 3, 0, (2, 1)), ("ff", 3, 0, (-1, -1)),
-    ("ff", 3, 1, (-1, -1)), ("gu", 2), ("fs", 0), ("rf", 1, 1, (1, 2)), ("rf", 1, 0, (1, 1)),
-    ("rf", 1, 1, (1, 1)), ("rf", 1, 0, (2, 1)), ("rf", 1, 0, (-1, -1)), ("rf", 1, 1, (-1, -1)), ("dn", 2, 2),
-    ("dn", 2, 1), ("dn", 2, -1), ("dn", 2, 0), ("ff", 4, 0, (1, 1)), ("ff", 4, 1, (1, 1)), ("fi", 0),
-    ("ff", 4, 1, (1, 2)), ("ff", 4, 0, (2, 1)), ("ff", 4, 0, (-1, -1)), ("ff", 4, 1, (-1, -1)),
-    ("rn", 1, (0, -1)), ("rn", 1, (-1, 0)), ("gu", 3), ("fs", 1), ("rf", 2, 1, (1, 2)), ("rf", 2, 0, (1, 1)),
-    ("rf", 2, 1, (1, 1)), ("rf", 2, 0, (2, 1)), ("rf", 2, 0, (-1, -1)), ("rf", 2, 1, (-1, -1)), ("dn", 3, 2),
-    ("dn", 3, 1), ("dn", 3, -1), ("rf", 2, 1, (0, 2)), ("dn", 3, 0), ("rf", 2, 0, (2, 0)), ("gu", 4),
-    ("rf", 3, 1, (1, 2)), ("rf", 3, 0, (1, 1)), ("rf", 3, 1, (1, 1)), ("rf", 3, 0, (2, 1)),
-    ("rf", 3, 0, (-1, -1)), ("rf", 3, 1, (-1, -1)), ("dn", 4, 2), ("dn", 4, 1), ("rf", 3, 1, (0, 2)),
-    ("dn", 4, -1), ("dn", 4, 0), ("rf", 3, 0, (2, 0)), ("fi", 1), ("rf", 4, 1, (1, 2)), ("rf", 4, 0, (1, 1)),
-    ("rf", 4, 1, (1, 1)), ("rf", 4, 0, (2, 1)), ("rf", 4, 0, (-1, -1)), ("rf", 4, 1, (-1, -1)),
-    ("rn", 2, (0, 1)), ("rn", 2, (0, -1)), ("rf", 4, 1, (0, 2)), ("rn", 2, (1, 0)), ("rn", 2, (-1, 0)),
-    ("rf", 4, 0, (2, 0)), ("rn", 3, (0, 1)), ("rn", 3, (0, -1)), ("rn", 3, (1, 0)), ("rn", 3, (-1, 0)),
-    ("l1", 0), ("rn", 4, (0, -1)), ("rn", 4, (-1, 0)), ("fi", 2), ("rn", 4, (0, 1)), ("rn", 4, (1, 0)),
-    ("fi", 3), ("l2", 0), ("l1", 1), ("fi", 4), ("l2", 1), ("co", 0), ("co", 2), ("co", 3), ("co", 1),
-    ("co", 4),
+    ("mq", 2), ("mq", 3), ("mq", 4), ("z", 0), ("fold",), ("mf", 2), ("uf", 0), ("mf", 3), ("mf", 4), ("z", 1),
+    ("z", 2), ("z", 3), ("fn", 0, (0, -1)), ("fn", 0, (-1, 0)), ("fn", 0, (1, 0)), ("fn", 0, (0, 1)), ("z", 4),
+    ("zx", 2), ("ff", 0, 1, (-1, -1)), ("uf", 1), ("ff", 0, 0, (-1, -1)), ("ff", 0, 0, (2, 0)),
+    ("ff", 0, 0, (1, 1)), ("uf", 2), ("ff", 0, 1, (1, 1)), ("ff", 0, 1, (0, 2)), ("zx", 3), ("zx", 4),
+    ("fn", 1, (0, 1)), ("fn", 1, (-1, 0)), ("fn", 1, (0, -1)), ("uf", 3), ("ff", 0, 0, (2, 1)),
+    ("fn", 1, (1, 0)), ("fn", 2, (1, 0)), ("uf", 4), ("fn", 2, (-1, 0)), ("fn", 2, (0, -1)),
+    ("ff", 0, 1, (1, 2)), ("fn", 2, (0, 1)), ("ff", 1, 1, (0, 2)), ("ff", 1, 1, (1, 1)), ("ff", 1, 0, (-1, -1)),
+    ("fn", 3, (0, 1)), ("fn", 3, (1, 0)), ("ff", 1, 1, (-1, -1)), ("fn", 3, (0, -1)), ("ff", 1, 0, (1, 1)),
+    ("ff", 1, 0, (2, 0)), ("fn", 3, (-1, 0)), ("ux", 2), ("fn", 4, (0, -1)), ("gu", 0), ("ff", 1, 1, (1, 2)),
+    ("ff", 1, 0, (2, 1)), ("dn", 0, 2), ("dn", 0, 1), ("dn", 0, -1), ("dn", 0, 0), ("ff", 2, 0, (1, 1)),
+    ("ff", 2, 1, (1, 1)), ("ff", 2, 0, (-1, -1)), ("ff", 2, 1, (-1, -1)), ("rn", 0, (0, 1)), ("rn", 0, (1, 0)),
+    ("fn", 4, (0, 1)), ("fn", 4, (1, 0)), ("fn", 4, (-1, 0)), ("ux", 3), ("ff", 2, 1, (1, 2)),
+    ("ff", 2, 0, (2, 1)), ("rf", 0, 1, (1, 2)), ("gu", 1), ("rf", 0, 0, (1, 1)), ("rf", 0, 1, (1, 1)),
+    ("rf", 0, 0, (2, 1)), ("rf", 0, 0, (-1, -1)), ("rf", 0, 1, (-1, -1)), ("dn", 1, 2), ("dn", 1, 1),
+    ("dn", 1, -1), ("dn", 1, 0), ("ff", 3, 0, (1, 1)), ("ff", 3, 1, (1, 1)), ("rn", 0, (0, -1)),
+    ("rn", 0, (-1, 0)), ("ff", 3, 0, (-1, -1)), ("ff", 3, 1, (-1, -1)), ("rn", 1, (0, 1)), ("rn", 1, (1, 0)),
+    ("ux", 4), ("ff", 3, 1, (1, 2)), ("ff", 3, 0, (2, 1)), ("gu", 2), ("rf", 1, 1, (1, 2)),
+    ("rf", 1, 0, (1, 1)), ("rf", 1, 1, (1, 1)), ("rf", 1, 0, (2, 1)), ("rf", 1, 0, (-1, -1)), ("dn", 2, 2),
+    ("dn", 2, 1), ("rf", 1, 1, (-1, -1)), ("dn", 2, -1), ("dn", 2, 0), ("fs", 0), ("rn", 1, (0, -1)),
+    ("ff", 4, 1, (1, 1)), ("ff", 4, 0, (1, 1)), ("rn", 1, (-1, 0)), ("rn", 2, (0, 1)), ("rn", 2, (1, 0)),
+    ("fi", 0), ("ff", 4, 1, (1, 2)), ("ff", 4, 0, (2, 1)), ("ff", 4, 0, (-1, -1)), ("ff", 4, 1, (-1, -1)),
+    ("gu", 3), ("rf", 2, 1, (1, 2)), ("rf", 2, 0, (1, 1)), ("rf", 2, 1, (1, 1)), ("rf", 2, 0, (2, 1)),
+    ("dn", 3, 2), ("rf", 2, 0, (-1, -1)), ("dn", 3, 1), ("rf", 2, 1, (-1, -1)), ("dn", 3, -1), ("dn", 3, 0),
+    ("fs", 1), ("gu", 4), ("rf", 3, 1, (1, 2)), ("rf", 3, 0, (1, 1)), ("rf", 3, 1, (1, 1)),
+    ("rf", 3, 0, (2, 1)), ("rf", 3, 0, (-1, -1)), ("dn", 4, 2), ("dn", 4, 1), ("rf", 3, 1, (-1, -1)),
+    ("dn", 4, -1), ("dn", 4, 0), ("fs", 2), ("rf", 4, 1, (1, 2)), ("rf", 4, 0, (1, 1)), ("rf", 4, 1, (1, 1)),
+    ("rf", 4, 0, (-1, -1)), ("rf", 4, 0, (2, 1)), ("rf", 3, 1, (0, 2)), ("rf", 4, 1, (-1, -1)),
+    ("rf", 3, 0, (2, 0)), ("rn", 2, (0, -1)), ("rn", 2, (-1, 0)), ("rn", 3, (0, -1)), ("rn", 3, (-1, 0)),
+    ("rf", 4, 1, (0, 2)), ("fi", 1), ("rf", 4, 0, (2, 0)), ("rn", 3, (0, 1)), ("rn", 3, (1, 0)), ("l1", 0),
+    ("rn", 4, (0, -1)), ("rn", 4, (-1, 0)), ("rn", 4, (0, 1)), ("rn", 4, (1, 0)), ("fi", 2), ("l1", 1),
+    ("fi", 3), ("l1", 2), ("l2", 0), ("fi", 4), ("l2", 1), ("l2", 2), ("co", 0), ("co", 3), ("co", 1),
+    ("co", 2), ("co", 4),
 )
 
 

time: 133 us -> 131 us (0.985)
  Pallas kernels: 131 us -> 129 us
    pallas_call x1, Pallas kernels: 131 us -> 129 us  [body(): pl.pallas_call(functools.partial(kernel, dims), out_shape=jax.ShapeDtypeS...]
where the time goes in v4:
time: 131 us
  Pallas kernels  129 us (98%)
  local copies, waits for them, and re-layouts  1.67 us (1%)
    pallas_call x1, Pallas kernels, body(): pl.pallas_call(functools.partial(kernel, dims), out_shape=jax.ShapeDtypeS...  129 us

profile of v4, /device:TPU:1, one launch (start us, length us, event | category | flops | bytes accessed | tf_op | source)
XLA Modules:
  0.0 130.6 jit_solution(10576655088703779533)
XLA Ops:
  0.0 129.0 %expert_block.1 = bf16[128,1024]{1,0:T(8,128)(2,1)} custom-call(bf16[128,1024]{1,0:T(8,128)(2,1)} %bitcast.20, s32[2,128]{1,0:T(2,128)} %bitcast.22, f32[2,128]{1,0:T(2,128)} %bitcast.23, f32[32,128]{1,0:T(8,128)} %bitcast.21, bf16[448,4096]{1,0:T(8,128)(2,1)} %bitcast.17, bf16[448,4096]{1,0:T(8,128)(2,1)} %bitcast.18, bf16[448,4096]{1,0:T(8,128)(2,1)} %bitcast.19), custom_call_target="tpu_custom_call" | custom-call | flops 14092861440 | bytes 11010048 | tf_op jit(solution)/shard_map/expert_block/pallas_call | solution.py:613
  129.0 1.7 %copy.9 = bf16[1,128,1024]{2,1,0:T(8,128)(2,1)} copy(bf16[1,128,1024]{2,1,0:T(8,128)(2,1)} %bitcast.16) | data formatting | bytes 524288

commit v5 on v4

--- a/solution.py
+++ b/solution.py
@@ -63,38 +63,38 @@
 SIDE_ID = {m: i for i, m in enumerate(SIDES)}
 
 ORDER = (
-    ("mq", 2), ("mq", 3), ("mq", 4), ("z", 0), ("fold",), ("mf", 2), ("uf", 0), ("mf", 3), ("mf", 4), ("z", 1),
-    ("z", 2), ("z", 3), ("fn", 0, (0, -1)), ("fn", 0, (-1, 0)), ("fn", 0, (1, 0)), ("fn", 0, (0, 1)), ("z", 4),
-    ("zx", 2), ("ff", 0, 1, (-1, -1)), ("uf", 1), ("ff", 0, 0, (-1, -1)), ("ff", 0, 0, (2, 0)),
-    ("ff", 0, 0, (1, 1)), ("uf", 2), ("ff", 0, 1, (1, 1)), ("ff", 0, 1, (0, 2)), ("zx", 3), ("zx", 4),
-    ("fn", 1, (0, 1)), ("fn", 1, (-1, 0)), ("fn", 1, (0, -1)), ("uf", 3), ("ff", 0, 0, (2, 1)),
-    ("fn", 1, (1, 0)), ("fn", 2, (1, 0)), ("uf", 4), ("fn", 2, (-1, 0)), ("fn", 2, (0, -1)),
-    ("ff", 0, 1, (1, 2)), ("fn", 2, (0, 1)), ("ff", 1, 1, (0, 2)), ("ff", 1, 1, (1, 1)), ("ff", 1, 0, (-1, -1)),
-    ("fn", 3, (0, 1)), ("fn", 3, (1, 0)), ("ff", 1, 1, (-1, -1)), ("fn", 3, (0, -1)), ("ff", 1, 0, (1, 1)),
-    ("ff", 1, 0, (2, 0)), ("fn", 3, (-1, 0)), ("ux", 2), ("fn", 4, (0, -1)), ("gu", 0), ("ff", 1, 1, (1, 2)),
-    ("ff", 1, 0, (2, 1)), ("dn", 0, 2), ("dn", 0, 1), ("dn", 0, -1), ("dn", 0, 0), ("ff", 2, 0, (1, 1)),
-    ("ff", 2, 1, (1, 1)), ("ff", 2, 0, (-1, -1)), ("ff", 2, 1, (-1, -1)), ("rn", 0, (0, 1)), ("rn", 0, (1, 0)),
-    ("fn", 4, (0, 1)), ("fn", 4, (1, 0)), ("fn", 4, (-1, 0)), ("ux", 3), ("ff", 2, 1, (1, 2)),
-    ("ff", 2, 0, (2, 1)), ("rf", 0, 1, (1, 2)), ("gu", 1), ("rf", 0, 0, (1, 1)), ("rf", 0, 1, (1, 1)),
-    ("rf", 0, 0, (2, 1)), ("rf", 0, 0, (-1, -1)), ("rf", 0, 1, (-1, -1)), ("dn", 1, 2), ("dn", 1, 1),
-    ("dn", 1, -1), ("dn", 1, 0), ("ff", 3, 0, (1, 1)), ("ff", 3, 1, (1, 1)), ("rn", 0, (0, -1)),
-    ("rn", 0, (-1, 0)), ("ff", 3, 0, (-1, -1)), ("ff", 3, 1, (-1, -1)), ("rn", 1, (0, 1)), ("rn", 1, (1, 0)),
-    ("ux", 4), ("ff", 3, 1, (1, 2)), ("ff", 3, 0, (2, 1)), ("gu", 2), ("rf", 1, 1, (1, 2)),
-    ("rf", 1, 0, (1, 1)), ("rf", 1, 1, (1, 1)), ("rf", 1, 0, (2, 1)), ("rf", 1, 0, (-1, -1)), ("dn", 2, 2),
-    ("dn", 2, 1), ("rf", 1, 1, (-1, -1)), ("dn", 2, -1), ("dn", 2, 0), ("fs", 0), ("rn", 1, (0, -1)),
-    ("ff", 4, 1, (1, 1)), ("ff", 4, 0, (1, 1)), ("rn", 1, (-1, 0)), ("rn", 2, (0, 1)), ("rn", 2, (1, 0)),
-    ("fi", 0), ("ff", 4, 1, (1, 2)), ("ff", 4, 0, (2, 1)), ("ff", 4, 0, (-1, -1)), ("ff", 4, 1, (-1, -1)),
-    ("gu", 3), ("rf", 2, 1, (1, 2)), ("rf", 2, 0, (1, 1)), ("rf", 2, 1, (1, 1)), ("rf", 2, 0, (2, 1)),
-    ("dn", 3, 2), ("rf", 2, 0, (-1, -1)), ("dn", 3, 1), ("rf", 2, 1, (-1, -1)), ("dn", 3, -1), ("dn", 3, 0),
-    ("fs", 1), ("gu", 4), ("rf", 3, 1, (1, 2)), ("rf", 3, 0, (1, 1)), ("rf", 3, 1, (1, 1)),
-    ("rf", 3, 0, (2, 1)), ("rf", 3, 0, (-1, -1)), ("dn", 4, 2), ("dn", 4, 1), ("rf", 3, 1, (-1, -1)),
-    ("dn", 4, -1), ("dn", 4, 0), ("fs", 2), ("rf", 4, 1, (1, 2)), ("rf", 4, 0, (1, 1)), ("rf", 4, 1, (1, 1)),
-    ("rf", 4, 0, (-1, -1)), ("rf", 4, 0, (2, 1)), ("rf", 3, 1, (0, 2)), ("rf", 4, 1, (-1, -1)),
-    ("rf", 3, 0, (2, 0)), ("rn", 2, (0, -1)), ("rn", 2, (-1, 0)), ("rn", 3, (0, -1)), ("rn", 3, (-1, 0)),
-    ("rf", 4, 1, (0, 2)), ("fi", 1), ("rf", 4, 0, (2, 0)), ("rn", 3, (0, 1)), ("rn", 3, (1, 0)), ("l1", 0),
-    ("rn", 4, (0, -1)), ("rn", 4, (-1, 0)), ("rn", 4, (0, 1)), ("rn", 4, (1, 0)), ("fi", 2), ("l1", 1),
-    ("fi", 3), ("l1", 2), ("l2", 0), ("fi", 4), ("l2", 1), ("l2", 2), ("co", 0), ("co", 3), ("co", 1),
-    ("co", 2), ("co", 4),
+    ("mq", 2), ("z", 0), ("mq", 3), ("mq", 4), ("z", 1), ("z", 2), ("mf", 2), ("mf", 3), ("z", 3), ("mf", 4),
+    ("uf", 0), ("zx", 2), ("uf", 1), ("zx", 3), ("z", 4), ("fn", 0, (1, 0)), ("fn", 0, (0, -1)),
+    ("fn", 0, (0, 1)), ("uf", 2), ("fn", 0, (-1, 0)), ("uf", 3), ("ff", 0, 0, (2, 0)), ("fn", 1, (0, 1)),
+    ("ff", 0, 0, (1, 1)), ("zx", 4), ("fn", 1, (1, 0)), ("ff", 0, 1, (0, 2)), ("fn", 1, (-1, 0)), ("fold",),
+    ("ff", 0, 0, (-1, -1)), ("fn", 2, (0, 1)), ("ff", 0, 1, (1, 1)), ("fn", 3, (1, 0)), ("fn", 2, (0, -1)),
+    ("ff", 0, 0, (2, 1)), ("fn", 3, (0, -1)), ("ff", 0, 1, (-1, -1)), ("ff", 0, 1, (1, 2)), ("fn", 2, (1, 0)),
+    ("ff", 1, 1, (1, 1)), ("fn", 2, (-1, 0)), ("ff", 1, 1, (0, 2)), ("ff", 1, 0, (2, 0)), ("fn", 3, (0, 1)),
+    ("fn", 3, (-1, 0)), ("ff", 1, 0, (1, 1)), ("fn", 1, (0, -1)), ("ux", 2), ("ff", 1, 0, (-1, -1)), ("gu", 0),
+    ("ff", 1, 0, (2, 1)), ("ff", 1, 1, (1, 2)), ("ff", 1, 1, (-1, -1)), ("ux", 3), ("dn", 0, 2), ("dn", 0, 1),
+    ("ff", 2, 1, (1, 1)), ("ff", 2, 0, (-1, -1)), ("ff", 2, 0, (1, 1)), ("ff", 2, 1, (1, 2)),
+    ("ff", 2, 0, (2, 1)), ("ff", 2, 1, (-1, -1)), ("uf", 4), ("gu", 1), ("ff", 3, 1, (1, 1)),
+    ("ff", 3, 0, (1, 1)), ("ff", 3, 0, (2, 1)), ("ff", 3, 0, (-1, -1)), ("ff", 3, 1, (1, 2)), ("ux", 4),
+    ("dn", 0, -1), ("ff", 3, 1, (-1, -1)), ("rf", 0, 0, (-1, -1)), ("dn", 1, 2), ("dn", 1, 1), ("dn", 1, -1),
+    ("dn", 0, 0), ("gu", 2), ("fn", 4, (0, -1)), ("ff", 4, 1, (-1, -1)), ("ff", 4, 0, (1, 1)),
+    ("rf", 0, 1, (1, 1)), ("rf", 0, 0, (1, 1)), ("rf", 0, 1, (1, 2)), ("rn", 0, (0, -1)), ("fn", 4, (0, 1)),
+    ("rf", 0, 0, (2, 1)), ("ff", 4, 0, (-1, -1)), ("dn", 1, 0), ("rf", 0, 1, (-1, -1)), ("ff", 4, 1, (1, 2)),
+    ("ff", 4, 1, (1, 1)), ("ff", 4, 0, (2, 1)), ("fn", 4, (-1, 0)), ("dn", 2, 2), ("gu", 3),
+    ("rf", 1, 0, (-1, -1)), ("rf", 1, 0, (1, 1)), ("rn", 1, (0, 1)), ("rf", 1, 1, (-1, -1)),
+    ("rf", 1, 1, (1, 1)), ("dn", 2, 1), ("rf", 1, 1, (1, 2)), ("rf", 1, 0, (2, 1)), ("rn", 1, (1, 0)),
+    ("dn", 2, -1), ("dn", 2, 0), ("rn", 2, (1, 0)), ("dn", 3, 2), ("dn", 3, 1), ("fs", 0), ("fn", 4, (1, 0)),
+    ("gu", 4), ("rf", 2, 0, (1, 1)), ("rn", 1, (0, -1)), ("rf", 2, 0, (-1, -1)), ("dn", 4, 2),
+    ("rf", 2, 1, (1, 2)), ("rn", 1, (-1, 0)), ("fs", 1), ("rf", 2, 1, (-1, -1)), ("rf", 2, 0, (2, 1)),
+    ("rn", 2, (0, -1)), ("dn", 3, -1), ("rf", 2, 1, (1, 1)), ("rn", 0, (-1, 0)), ("rn", 2, (-1, 0)),
+    ("dn", 4, 1), ("dn", 4, -1), ("rn", 2, (0, 1)), ("rf", 3, 0, (-1, -1)), ("rf", 3, 0, (2, 1)),
+    ("rf", 4, 0, (2, 1)), ("rn", 0, (0, 1)), ("rf", 4, 1, (1, 2)), ("fi", 1), ("rf", 3, 1, (1, 2)),
+    ("rf", 3, 1, (-1, -1)), ("dn", 4, 0), ("fs", 2), ("dn", 3, 0), ("rf", 4, 1, (1, 1)), ("rf", 4, 1, (0, 2)),
+    ("rf", 4, 0, (1, 1)), ("rn", 0, (1, 0)), ("rf", 3, 0, (1, 1)), ("l1", 0), ("rf", 4, 0, (-1, -1)), ("fi", 2),
+    ("rf", 4, 1, (-1, -1)), ("rf", 3, 0, (2, 0)), ("rn", 3, (0, -1)), ("rf", 4, 0, (2, 0)), ("rn", 4, (0, 1)),
+    ("rf", 3, 1, (0, 2)), ("rf", 3, 1, (1, 1)), ("l1", 1), ("rn", 4, (0, -1)), ("rn", 4, (-1, 0)),
+    ("rn", 4, (1, 0)), ("rn", 3, (1, 0)), ("rn", 3, (0, 1)), ("rn", 3, (-1, 0)), ("fi", 0), ("l1", 2),
+    ("l2", 0), ("fi", 4), ("l2", 1), ("fi", 3), ("l2", 2), ("co", 0), ("co", 1), ("co", 4), ("co", 2),
+    ("co", 3),
 )
 
 

time: 131 us -> 130 us (level)
  no operation moved by 1% of the time
where the time goes in v5:
time: 130 us
  Pallas kernels  129 us (99%)
  local copies, waits for them, and re-layouts  1.67 us (1%)
    pallas_call x1, Pallas kernels, body(): pl.pallas_call(functools.partial(kernel, dims), out_shape=jax.ShapeDtypeS...  129 us

profile of v5, /device:TPU:1, one launch (start us, length us, event | category | flops | bytes accessed | tf_op | source)
XLA Modules:
  0.0 130.3 jit_solution(15532195496832473339)
XLA Ops:
  0.0 128.6 %expert_block.1 = bf16[128,1024]{1,0:T(8,128)(2,1)} custom-call(bf16[128,1024]{1,0:T(8,128)(2,1)} %bitcast.20, s32[2,128]{1,0:T(2,128)} %bitcast.22, f32[2,128]{1,0:T(2,128)} %bitcast.23, f32[32,128]{1,0:T(8,128)} %bitcast.21, bf16[448,4096]{1,0:T(8,128)(2,1)} %bitcast.17, bf16[448,4096]{1,0:T(8,128)(2,1)} %bitcast.18, bf16[448,4096]{1,0:T(8,128)(2,1)} %bitcast.19), custom_call_target="tpu_custom_call" | custom-call | flops 14092861440 | bytes 11010048 | tf_op jit(solution)/shard_map/expert_block/pallas_call | solution.py:613
  128.6 1.7 %copy.9 = bf16[1,128,1024]{2,1,0:T(8,128)(2,1)} copy(bf16[1,128,1024]{2,1,0:T(8,128)(2,1)} %bitcast.16) | data formatting | bytes 524288
